TPU v7x, 32 devices: a whole 2x2x4 slice. The times are simulated.
32 devices in a mesh: blk: 4 (over x, core), rep: 8 (over z, y).
Axes of the slice: x: 2, y: 2, z: 4, core: 2. Of those that a mesh axis runs over, the one named last changes fastest.
Arguments:
- features: bfloat16 [64, 128, 256], P(('blk', 'rep')), may hold values from -6 to 6
- weight: bfloat16 [256, 256], replicated, may hold values from -0.375 to 0.375
- tile_values: bfloat16 [64, 8, 128, 128], P(('blk', 'rep')), may hold values from -0.1875 to 0.1875
- tile_count: int32 [64], P(('blk', 'rep')), may hold values from 1 to 8, as said below
- tile_cols: int32 [64, 8], P(('blk', 'rep')), may hold values from 0 to 63, as said below
- out_grad: bfloat16 [64, 128, 256], P(('blk', 'rep')), may hold values from -6 to 6
- relu_mask: int32 [64, 128, 256], P(('blk', 'rep')), may hold values 0 or 1
Outputs:
- activated: bfloat16 [64, 128, 256], P(('blk', 'rep'))
- weight_grad: float32 [256, 256], replicated
- in_grad: bfloat16 [64, 128, 256], P(('blk', 'rep'))
Inputs may be any that keep to these rules, and one draw needn't show every extreme that they name: `tile_count`: all 2 tile rows of some aligned block of 2 tile rows hold 8 tiles; some tile row holds one. `tile_cols`: tile rows form 8 communities: tile row t belongs to community t // 2 % 8, and every column tile of a tile row lies in its own community; the 8 column tiles of one tile row are distinct; slots not in use hold column tiles too.
All inputs are finite; a program needn't handle non-finite values. No bound on the sum of `relu_mask` on one device may be relied on, other than what follows from the above.
Results may differ from a plain program's by a relative error of at most 0.0049.
Values may be sent and summed in bfloat16 or wider, within the bound.
A program may use at most 64 MiB of HBM per device.

v0:
```python
import math

import jax
import jax.numpy as jnp
from jax import lax
from jax.sharding import PartitionSpec as P


def per_device(features, weight, tile_values, tile_count, tile_cols, out_grad, relu_mask):
    row_tiles = tile_values.shape[0]
    slot_count = tile_values.shape[1]
    tile_size = tile_values.shape[2]
    feature_width = features.shape[2]
    blk_size = lax.axis_size("blk")
    rep_size = lax.axis_size("rep")
    community = blk_size * row_tiles
    local_cols = tile_cols // (rep_size * row_tiles) * row_tiles + tile_cols % row_tiles
    in_use = lax.broadcasted_iota(jnp.int32, (row_tiles, slot_count), 1) < tile_count[:, None]
    member_ids = lax.broadcasted_iota(jnp.int32, (row_tiles, slot_count, community), 2)
    one_hot = ((local_cols[:, :, None] == member_ids) & in_use[:, :, None]).astype(jnp.bfloat16)
    selected = jnp.einsum(
        "tsc,tsji->tcji", one_hot, tile_values, preferred_element_type=jnp.float32
    ).astype(jnp.bfloat16)
    gathered = lax.all_gather(features, "blk", axis=0, tiled=True)
    picked = gathered[local_cols]
    picked = jnp.where(in_use[:, :, None, None], picked, jnp.zeros((), jnp.bfloat16))
    partial_value = jnp.einsum(
        "tsji,tsjf->tif", tile_values, picked, preferred_element_type=jnp.float32
    )
    hidden = partial_value.astype(jnp.bfloat16)
    hidden_flat = hidden.reshape(-1, feature_width)
    linear = jnp.dot(hidden_flat, weight, preferred_element_type=jnp.float32)
    activated = jnp.maximum(linear, 0.0).astype(jnp.bfloat16).reshape(hidden.shape)
    grad_flat = out_grad.reshape(-1, feature_width)
    grad_term = lax.dot_general(
        hidden_flat, grad_flat, (((0,), (0,)), ((), ())), preferred_element_type=jnp.float32
    )
    node_count = row_tiles * blk_size * rep_size * tile_size
    weight_grad = lax.psum(grad_term, ("blk", "rep")) * (1.0 / math.sqrt(node_count))
    row_grad = lax.dot_general(
        grad_flat, weight, (((1,), (1,)), ((), ())), preferred_element_type=jnp.float32
    )
    row_grad = row_grad.astype(jnp.bfloat16).reshape(out_grad.shape)
    spread = lax.psum_scatter(
        jnp.einsum("tcji,tif->cjf", selected, row_grad, preferred_element_type=jnp.float32),
        "blk",
        scatter_dimension=0,
        tiled=True,
    )
    in_grad = (relu_mask.astype(jnp.float32) * spread).astype(jnp.bfloat16)
    return (activated, weight_grad, in_grad)


def solution(mesh):
    placed = (
        P(("blk", "rep"), None, None),
        P(),
        P(("blk", "rep"), None, None, None),
        P(("blk", "rep")),
        P(("blk", "rep"), None),
        P(("blk", "rep"), None, None),
        P(("blk", "rep"), None, None),
    )
    return jax.shard_map(
        per_device,
        mesh=mesh,
        in_specs=placed,
        out_specs=(P(("blk", "rep"), None, None), P(), P(("blk", "rep"), None, None)),
        check_vma=False,
    )
```

profile of v0, /device:TPU:0, one launch (start us, length us, event | category | flops | bytes accessed | tf_op | source)
XLA Modules:
  0.0 157.0 jit_solution(4700501808886215289)
XLA Ops:
  8.0 0.0 copy-start
  8.0 0.0 copy-start.4
  8.0 0.0 all-reduce.2.cloned.1.call-start
  8.1 0.8 iota_compare_fusion.1
  8.8 0.0 copy-done.4
  8.9 0.1 reshape.61
  9.0 8.8 %all_gather.3 = bf16[8,128,256]{2,1,0:T(8,128)(2,1)S(1)} all-gather(bf16[2,128,256]{2,1,0:T(8,128)(2,1)} %param.7), channel_id=1, replica_groups=mesh['blk'=4,'rep'=8] {'blk'}, dimensions={0}, use_global_device_ids=true | all-gather | bytes 655360 | tf_op jit(solution)/shard_map/all_gather | solution.py:24
  17.8 0.6 gather_fusion
  18.4 0.0 copy-done
  18.4 0.0 copy-start.2
  18.4 0.4 fusion.1
  18.8 0.5 copy-done.2
  19.3 0.9 convolution_bitcast_fusion.1
  20.2 0.0 all-reduce.2.cloned.1.call-update
  20.3 0.0 reduce-scatter.2.cloned.1.call-start
  20.3 0.0 copy-start.1
  20.3 0.5 fusion.4
  20.8 0.4 copy-done.1
  21.2 0.2 convolution_convert_fusion
  21.4 1.3 convolution_bitcast_fusion
  22.7 0.0 reduce-scatter.2.cloned.1.call-update
  22.8 0.8 fusion
  23.6 0.0 copy-start.3
  23.6 122.7 %all-reduce.2.cloned.1.call-done = f32[256,256]{1,0:T(8,128)} async-done(((f32[256,256]{1,0:T(8,128)}), f32[256,256]{1,0:T(8,128)}) %all-reduce.2.cloned.1.call-update) | async-done | bytes 262160 | tf_op jit(solution)/shard_map/psum | solution.py:39
  146.3 1.7 %broadcast_multiply_fusion = f32[256,256]{1,0:T(8,128)} fusion(f32[256,256]{1,0:T(8,128)} %all-reduce.2.cloned.1.call-done), kind=kLoop, calls=%fused_computation.16 | loop fusion | flops 65536 | bytes 524288 | tf_op jit(solution)/shard_map/mul | solution.py:39
  147.9 0.0 reduce-scatter.2.cloned.1.call-done
  147.9 0.0 copy-done.3
  147.9 1.6 %multiply_convert_fusion = bf16[2,128,256]{2,1,0:T(8,128)(2,1)} fusion(f32[2,128,256]{2,1,0:T(8,128)} %reduce-scatter.2.cloned.1.call-done, s32[2,128,256]{2,1,0:T(8,128)S(1)} %copy-done.3), kind=kLoop, calls=%fused_computation.14 | loop fusion | flops 196608 | bytes 655360 | tf_op jit(solution)/shard_map/convert_element_type | solution.py:50
  (2 shorter events, 0.0 us)
Async XLA Ops:
  8.0 10.4 %copy-start = (bf16[2,8,128,128]{3,2,1,0:T(8,128)(2,1)S(1)}, bf16[2,8,128,128]{3,2,1,0:T(8,128)(2,1)}, u32[]{:S(2)}) copy-start(bf16[2,8,128,128]{3,2,1,0:T(8,128)(2,1)} %param.9) | copy-start | bytes 1572868
  8.0 0.8 copy-start.4
  8.0 138.2 %all-reduce.2.cloned.1.call-start = ((), (), s32[]{:S(2)}) async-start(), calls=%async_computation.1 | async-start | bytes 524288 | tf_op jit(solution)/shard_map/psum | solution.py:39
  18.4 0.9 copy-start.2
  20.3 127.7 %reduce-scatter.2.cloned.1.call-start = ((), (), s32[]{:S(2)}) async-start(), calls=%async_computation.2 | async-start | bytes 1310720 | tf_op jit(solution)/shard_map/reduce_scatter | solution.py:44
  20.3 0.9 copy-start.1
  23.6 124.3 %copy-start.3 = (s32[2,128,256]{2,1,0:T(8,128)S(1)}, s32[2,128,256]{2,1,0:T(8,128)}, u32[]{:S(2)}) copy-start(s32[2,128,256]{2,1,0:T(8,128)} %param.13) | copy-start | bytes 786436
Sparse Core Ops, SparseCore 0:
  20.4 125.8 all-reduce.1
Sparse Core Ops, SparseCore 1:
  23.3 25.7 reduce-scatter.1
where the time goes:
time: 157 us
  waiting for transfers between devices  123 us (78%)
  between operations  15.5 us (10%)
  blocking collectives  8.82 us (6%)
  matrix products  4.17 us (3%)
  other arithmetic  4.11 us (3%)
  local copies, waits for them, and re-layouts  1.61 us (1%)
    psum x1, waiting for transfers between devices, per_device(): lax.psum(grad_term, ('blk', 'rep')) * (1.0 / math.sqrt(node_count))  123 us
    all_gather x1, blocking collectives, per_device(): gathered = lax.all_gather(features, 'blk', axis=0, tiled=True)  8.82 us
  transfers between devices with their start and end apart: 2, of which 1 were waited for; matrix products, arithmetic and copies ran while one was open for 3% of the time, Pallas kernels for 0%

commit v1 on v0

v1 whole, which is shorter than its diff:
```python
import functools
import math

import jax
import jax.numpy as jnp
from jax import lax
from jax.experimental import pallas as pl
from jax.experimental.pallas import tpu as pltpu
from jax.sharding import PartitionSpec as P

MESH = pl.DeviceIdType.MESH
BF16 = jnp.bfloat16
F32 = jnp.float32


def each(count, body):
    if count <= 2:
        for step in range(count):
            body(step)
    else:
        lax.fori_loop(0, count, lambda step, carry: (body(step), carry)[1], 0)


def dot(a, b, contract=((1,), (0,))):
    return lax.dot_general(a, b, (contract, ((), ())), preferred_element_type=F32)


def kernel(dims, *refs):
    blk_size, rep_size, rows_per, slots, tile, width, plane_y, reduce_in = dims
    (count_ref, cols_ref, feat_ref, tv_ref, grad_ref, weight_ref) = refs[:6]
    (act_ref, col_ref, wg_ref) = refs[6:9]
    (tv, grad, weight, feats, mt, rg, own, one_send, one_recv, two_send, two_recv,
     act, col, wg_part, rs_recv, z_buf, wg_full,
     in_sem, out_sem, f_send, f_recv, fwd_send, one_ssem, one_rsem, two_ssem, two_rsem,
     rs_ssem, rs_rsem, z_ssem, z_rsem, ag_ssem, ag_rsem) = refs[9:]
    nodes = rows_per * tile
    chips = blk_size // 2
    z_size = rep_size // plane_y
    plane = blk_size * plane_y
    blk, rep = lax.axis_index("blk"), lax.axis_index("rep")
    chip, core = blk // 2, lax.rem(blk, 2)
    sib = chip * 2 + 1 - core
    my_y, my_z = lax.rem(rep, plane_y), rep // plane_y
    place = my_y * blk_size + blk

    def other_chip(step):
        return lax.rem(chip + 1 + step, chips)

    def plane_id(step):
        there = lax.rem(place + step, plane)
        return there, {"blk": lax.rem(there, blk_size), "rep": my_z * plane_y + there // blk_size}

    def z_id(step):
        there = lax.rem(my_z + step, z_size)
        return there, {"blk": blk, "rep": there * plane_y + my_y}

    loads = [pltpu.make_async_copy(grad_ref, grad, in_sem.at[0]),
             pltpu.make_async_copy(weight_ref, weight, in_sem.at[1])]
    for t in range(rows_per):
        loads.append(pltpu.make_async_copy(tv_ref.at[t], tv.at[t, pl.ds(0, slots)], in_sem.at[2 + t]))
    my_rows = pl.ds(pl.multiple_of(core * nodes, nodes), nodes)
    sib_rows = pl.ds(pl.multiple_of((1 - core) * nodes, nodes), nodes)
    loads.append(pltpu.make_async_copy(feat_ref, feats.at[chip, my_rows], in_sem.at[2 + rows_per]))
    for load in loads:
        load.start()

    barrier = pltpu.get_barrier_semaphore()
    if reduce_in:
        for step in range(1, plane):
            pl.semaphore_signal(barrier, inc=1, device_id=plane_id(step)[1], device_id_type=MESH)
        for step in range(1, z_size):
            pl.semaphore_signal(barrier, inc=1, device_id=z_id(step)[1], device_id_type=MESH)
        greeted = plane - 1 + z_size - 1
    else:
        pl.semaphore_signal(barrier, inc=1, device_id={"blk": sib, "rep": rep}, device_id_type=MESH)
        for step in range(chips - 1):
            pl.semaphore_signal(
                barrier, inc=1, device_id={"blk": other_chip(step) * 2 + core, "rep": rep}, device_id_type=MESH)
        greeted = chips
    loads[0].wait()
    loads[1].wait()
    rg[...] = dot(grad[...], weight[...], ((1,), (1,))).astype(BF16)
    pl.semaphore_wait(barrier, greeted)

    def send_x(step, piece):
        q = other_chip(step)
        rows = pl.ds(pl.multiple_of(core * nodes + piece * tile, tile), tile)
        return pltpu.make_async_remote_copy(
            src_ref=feat_ref.at[pl.ds(piece * tile, tile)], dst_ref=feats.at[chip, rows],
            send_sem=f_send.at[q, piece], recv_sem=f_recv.at[0, chip, piece],
            device_id={"blk": q * 2 + core, "rep": rep}, device_id_type=MESH)

    def came_x(q, piece):
        rows = pl.ds(pl.multiple_of(core * nodes + piece * tile, tile), tile)
        return pltpu.make_async_remote_copy(
            src_ref=feat_ref.at[pl.ds(piece * tile, tile)], dst_ref=feats.at[q, rows],
            send_sem=f_send.at[q, piece], recv_sem=f_recv.at[0, q, piece],
            device_id={"blk": q * 2 + core, "rep": rep}, device_id_type=MESH)

    def pass_on(q, piece):
        rows = pl.ds(pl.multiple_of(core * nodes + piece * tile, tile), tile)
        return pltpu.make_async_remote_copy(
            src_ref=feats.at[q, rows], dst_ref=feats.at[q, rows],
            send_sem=fwd_send.at[q, piece], recv_sem=f_recv.at[1, q, piece],
            device_id={"blk": sib, "rep": rep}, device_id_type=MESH)

    def passed(q, piece):
        rows = pl.ds(pl.multiple_of((1 - core) * nodes + piece * tile, tile), tile)
        return pltpu.make_async_remote_copy(
            src_ref=feats.at[q, rows], dst_ref=feats.at[q, rows],
            send_sem=fwd_send.at[q, piece], recv_sem=f_recv.at[1, q, piece],
            device_id={"blk": sib, "rep": rep}, device_id_type=MESH)

    for piece in range(rows_per):
        each(chips - 1, lambda step: send_x(step, piece).start())
    loads[-1].wait()
    for piece in range(rows_per):
        pass_on(chip, piece).start()

    for t in range(rows_per):
        loads[2 + t].wait()
        tv[t, slots] = jnp.zeros((tile, tile), BF16)

    def block_of(q, c):
        member = q * 2 + c
        bands = []
        for r in range(rows_per):
            column = (member * rep_size + rep) * rows_per + r
            pieces = []
            for t in range(rows_per):
                slot = jnp.int32(slots)
                for s in range(slots):
                    hit = jnp.logical_and(cols_ref[t, s] == column, s < count_ref[t])
                    slot = jnp.where(hit, jnp.int32(s), slot)
                pieces.append(tv[t, slot])
            bands.append(jnp.concatenate(pieces, axis=1))
        return jnp.concatenate(bands, axis=0)

    def one_copy(q):
        return pltpu.make_async_remote_copy(
            src_ref=one_send.at[q], dst_ref=one_recv.at[q],
            send_sem=one_ssem.at[q], recv_sem=one_rsem.at[q],
            device_id={"blk": sib, "rep": rep}, device_id_type=MESH)

    def two_copy(q, slot):
        return pltpu.make_async_remote_copy(
            src_ref=two_send.at[q], dst_ref=two_recv.at[slot],
            send_sem=two_ssem.at[q], recv_sem=two_rsem.at[slot],
            device_id={"blk": q * 2 + core, "rep": rep}, device_id_type=MESH)

    def for_sibling(step):
        q = other_chip(step)
        block = block_of(q, 1 - core)
        one_send[q] = dot(block, rg[...]).astype(BF16)
        one_copy(q).start()
        mt[q, :, sib_rows] = block.T

    def for_core(step):
        q = other_chip(step)
        block = block_of(q, core)
        own[q] = dot(block, rg[...])
        mt[q, :, my_rows] = block.T

    each(chips, for_sibling)
    each(chips, for_core)

    def second(step):
        q = other_chip(step)
        one_copy(q).wait_recv()
        two_send[q] = (own[q] + one_recv[q].astype(F32)).astype(BF16)
        two_copy(q, chip).start()

    def hand_on(step):
        q = other_chip(step)
        for piece in range(rows_per):
            came_x(q, piece).wait_recv()
            pass_on(q, piece).start()

    each(chips - 1, second)
    each(chips - 1, hand_on)

    for piece in range(rows_per):
        passed(chip, piece).wait_recv()
    own_part = dot(mt[chip], feats[chip])
    act[...] = own_part

    def forward(step):
        q = other_chip(step)
        for piece in range(rows_per):
            passed(q, piece).wait_recv()
        act[...] += dot(mt[q], feats[q])

    each(chips - 1, forward)
    hidden = act[...].astype(BF16)
    term = dot(hidden, grad[...], ((0,), (0,)))

    if reduce_in:
        share = width // plane
        wg_part[...] = term.astype(BF16)

        def rs_copy(step):
            there, device = plane_id(step)
            return pltpu.make_async_remote_copy(
                src_ref=wg_part.at[pl.ds(pl.multiple_of(there * share, share), share)],
                dst_ref=rs_recv.at[step - 1],
                send_sem=rs_ssem.at[step - 1], recv_sem=rs_rsem.at[step - 1],
                device_id=device, device_id_type=MESH)

        for step in range(1, plane):
            rs_copy(step).start()
    else:
        wg_ref[...] = term

    act_ref[...] = dot(hidden, weight[...]).astype(BF16)
    one_copy(chip).wait_recv()
    col[...] = own[chip] + one_recv[chip].astype(F32)

    def gathered(step):
        q = other_chip(step)
        two_copy(q, q).wait_recv()
        col[...] += two_recv[q].astype(F32)

    each(chips - 1, gathered)
    col_ref[...] = col[...].astype(BF16)

    if reduce_in:
        my_share = pl.ds(pl.multiple_of(place * share, share), share)
        total = wg_part[my_share].astype(F32)
        for step in range(1, plane):
            rs_copy(step).wait_recv()
            total = total + rs_recv[step - 1].astype(F32)
        z_buf[my_z] = total.astype(BF16)

        def z_copy(step, slot):
            return pltpu.make_async_remote_copy(
                src_ref=z_buf.at[my_z], dst_ref=z_buf.at[slot],
                send_sem=z_ssem.at[step - 1], recv_sem=z_rsem.at[slot],
                device_id=z_id(step)[1], device_id_type=MESH)

        for step in range(1, z_size):
            z_copy(step, my_z).start()
        for step in range(1, z_size):
            z_copy(step, z_id(step)[0]).wait_recv()
        total = z_buf[0].astype(F32)
        for z in range(1, z_size):
            total = total + z_buf[z].astype(F32)
        scale = 1.0 / math.sqrt(nodes * blk_size * rep_size)
        wg_full[my_share] = (total * scale).astype(BF16)

        def ag_copy(step, owner):
            rows = pl.ds(pl.multiple_of(owner * share, share), share)
            return pltpu.make_async_remote_copy(
                src_ref=wg_full.at[rows], dst_ref=wg_full.at[rows],
                send_sem=ag_ssem.at[step - 1], recv_sem=ag_rsem.at[step - 1],
                device_id=plane_id(step)[1], device_id_type=MESH)

        for step in range(1, plane):
            ag_copy(step, place).start()
        for step in range(1, plane):
            ag_copy(step, lax.rem(place + plane - step, plane)).wait_recv()
        wg_ref[...] = wg_full[...].astype(F32)

    for piece in range(rows_per):
        each(chips - 1, lambda step: send_x(step, piece).wait_send())
        each(chips, lambda step: pass_on(other_chip(step), piece).wait_send())
    each(chips, lambda step: one_copy(other_chip(step)).wait_send())
    each(chips - 1, lambda step: two_copy(other_chip(step), chip).wait_send())
    if reduce_in:
        for step in range(1, plane):
            rs_copy(step).wait_send()
            ag_copy(step, place).wait_send()
        for step in range(1, z_size):
            z_copy(step, my_z).wait_send()


def per_device(features, weight, tile_values, tile_count, tile_cols, out_grad, relu_mask):
    rows_per, slots, tile = tile_values.shape[:3]
    width = features.shape[2]
    nodes = rows_per * tile
    blk_size, rep_size = lax.axis_size("blk"), lax.axis_size("rep")
    chips = blk_size // 2
    plane_y = 2
    z_size = rep_size // plane_y
    plane = blk_size * plane_y
    reduce_in = width % (plane * 16) == 0 and z_size <= 8
    share = width // plane if reduce_in else 16
    block = (nodes, width)
    dma = pltpu.SemaphoreType.DMA
    vmem = pltpu.VMEM
    scratch = [
        vmem((rows_per, slots + 1, tile, tile), BF16),
        vmem(block, BF16),
        vmem((width, width), BF16),
        vmem((chips, 2 * nodes, width), BF16),
        vmem((chips, nodes, 2 * nodes), BF16),
        vmem(block, BF16),
        vmem((chips,) + block, F32),
        vmem((chips,) + block, BF16),
        vmem((chips,) + block, BF16),
        vmem((chips,) + block, BF16),
        vmem((chips,) + block, BF16),
        vmem(block, F32),
        vmem(block, F32),
        vmem((width, width), BF16),
        vmem((plane - 1, share, width), BF16),
        vmem((z_size, share, width), BF16),
        vmem((width, width), BF16),
        dma((3 + rows_per,)), dma((2,)),
        dma((chips, rows_per)), dma((2, chips, rows_per)), dma((chips, rows_per)),
        dma((chips,)), dma((chips,)), dma((chips,)), dma((chips,)),
        dma((plane - 1,)), dma((plane - 1,)), dma((z_size,)), dma((z_size,)),
        dma((plane - 1,)), dma((plane - 1,)),
    ]
    smem = pl.BlockSpec(memory_space=pltpu.SMEM)
    hbm = pl.BlockSpec(memory_space=pl.ANY)
    whole = pl.BlockSpec(memory_space=pltpu.VMEM)
    dims = (blk_size, rep_size, rows_per, slots, tile, width, plane_y, reduce_in)
    linear, column, weight_term = pl.pallas_call(
        functools.partial(kernel, dims),
        out_shape=(
            jax.ShapeDtypeStruct(block, BF16),
            jax.ShapeDtypeStruct(block, BF16),
            jax.ShapeDtypeStruct((width, width), F32),
        ),
        in_specs=[smem, smem, hbm, hbm, hbm, hbm],
        out_specs=(whole, whole, whole),
        scratch_shapes=scratch,
        compiler_params=pltpu.CompilerParams(
            collective_id=0, has_side_effects=True, vmem_limit_bytes=32 * 1024 * 1024
        ),
        name="layer",
    )(tile_count, tile_cols, features.reshape(block), tile_values, out_grad.reshape(block), weight)
    activated = jnp.maximum(linear, 0).reshape(features.shape)
    in_grad = jnp.where(relu_mask != 0, column.reshape(features.shape), jnp.zeros((), BF16))
    if not reduce_in:
        scale = 1.0 / math.sqrt(nodes * blk_size * rep_size)
        weight_term = lax.psum(weight_term, ("blk", "rep")) * scale
    return (activated, weight_term, in_grad)


def solution(mesh):
    placed = (
        P(("blk", "rep"), None, None),
        P(),
        P(("blk", "rep"), None, None, None),
        P(("blk", "rep")),
        P(("blk", "rep"), None),
        P(("blk", "rep"), None, None),
        P(("blk", "rep"), None, None),
    )
    return jax.shard_map(
        per_device,
        mesh=mesh,
        in_specs=placed,
        out_specs=(P(("blk", "rep"), None, None), P(), P(("blk", "rep"), None, None)),
        check_vma=False,
    )
```

time: 157 us -> 31.7 us (0.20)
  waiting for transfers between devices: 123 us -> 0 us
  Pallas kernels: 0 us -> 24 us
  between operations: 15.5 us -> 0.67 us
  blocking collectives: 8.82 us -> 0 us
  matrix products: 4.17 us -> 0 us
  local copies, waits for them, and re-layouts: 1.61 us -> 5.45 us
  other arithmetic: 4.11 us -> 1.36 us
    psum x1 -> x0, waiting for transfers between devices: 123 us -> none  [per_device(): lax.psum(grad_term, ('blk', 'rep')) * (1.0 / math.sqrt(node_count))]
    pallas_call x0 -> x1, Pallas kernels: none -> 24 us  [per_device(): pl.pallas_call(functools.partial(kernel, dims), out_shape=(jax.ShapeDtype...]
    all_gather x1 -> x0, blocking collectives: 8.82 us -> none  [per_device(): gathered = lax.all_gather(features, 'blk', axis=0, tiled=True)]
    unnamed x10 -> x15, local copies, waits for them, and re-layouts: 0.91 us -> 5.45 us
    dot_general x6 -> x0, matrix products: 4.17 us -> none  [the longest x1 1.28 us: per_device(): jnp.einsum('tcji,tif->cjf', selected, row_grad, preferred_element_type=jn...]
    mul x1 -> x0, other arithmetic: 1.68 us -> none  [per_device(): lax.psum(grad_term, ('blk', 'rep')) * (1.0 / math.sqrt(node_count))]
    convert_element_type x1 -> x0, other arithmetic: 1.64 us -> none  [per_device(): in_grad = (relu_mask.astype(jnp.float32) * spread).astype(jnp.bfloat16)]
  transfers between devices with their start and end apart: 2 -> 0, of which waited for: 1 -> 0; matrix products, arithmetic and copies ran while one was open for 3% -> 0% of each run, Pallas kernels for 0% -> 0%
where the time goes in v1:
time: 31.7 us; the launch traced here: 31.5 us
  Pallas kernels  24 us (76%)
  local copies, waits for them, and re-layouts  5.45 us (17%)
  other arithmetic  1.36 us (4%)
  between operations  0.67 us (2%)
    pallas_call x1, Pallas kernels, per_device(): pl.pallas_call(functools.partial(kernel, dims), out_shape=(jax.ShapeDtype...  24 us
    unnamed x15, local copies, waits for them, and re-layouts  5.45 us
    select_n x1, other arithmetic, per_device(): jnp.where(relu_mask != 0, column.reshape(features.shape), jnp.zeros((), B...  0.69 us
    max x1, other arithmetic, per_device(): activated = jnp.maximum(linear, 0).reshape(features.shape)  0.67 us

profile of v1, /device:TPU:0, one launch (start us, length us, event | category | flops | bytes accessed | tf_op | source)
XLA Modules:
  0.0 31.5 jit_solution(9335675317218333489)
XLA Ops:
  0.6 0.0 copy-start.4
  0.6 0.0 copy-start.5
  0.7 0.7 %copy-done.4 = s32[2,8]{1,0:T(2,128)S(1)} copy-done((s32[2,8]{1,0:T(2,128)S(1)}, s32[2,8]{1,0:T(2,128)}, u32[]{:S(2)}) %copy-start.4) | copy-done | bytes 88
  1.3 0.0 copy-done.5
  1.3 0.0 copy-start
  1.3 1.0 %copy-done = bf16[2,8,128,128]{3,2,1,0:T(8,128)(2,1)S(1)} copy-done((bf16[2,8,128,128]{3,2,1,0:T(8,128)(2,1)S(1)}, bf16[2,8,128,128]{3,2,1,0:T(8,128)(2,1)}, u32[]{:S(2)}) %copy-start) | copy-done | bytes 524312
  2.4 0.0 copy-start.1
  2.4 0.9 %copy-done.1 = bf16[2,128,256]{2,1,0:T(8,128)(2,1)S(1)} copy-done((bf16[2,128,256]{2,1,0:T(8,128)(2,1)S(1)}, bf16[2,128,256]{2,1,0:T(8,128)(2,1)}, u32[]{:S(2)}) %copy-start.1) | copy-done | bytes 131096
  3.3 0.0 copy-start.2
  3.3 0.9 %copy-done.2 = bf16[2,128,256]{2,1,0:T(8,128)(2,1)S(1)} copy-done((bf16[2,128,256]{2,1,0:T(8,128)(2,1)S(1)}, bf16[2,128,256]{2,1,0:T(8,128)(2,1)}, u32[]{:S(2)}) %copy-start.2) | copy-done | bytes 131096
  4.2 0.0 copy-start.3
  4.2 0.9 %copy-done.3 = bf16[256,256]{1,0:T(8,128)(2,1)S(1)} copy-done((bf16[256,256]{1,0:T(8,128)(2,1)S(1)}, bf16[256,256]{1,0:T(8,128)(2,1)}, u32[]{:S(2)}) %copy-start.3) | copy-done | bytes 131096
  5.1 24.0 %layer.1 = (bf16[256,256]{1,0:T(8,128)(2,1)S(1)}, bf16[256,256]{1,0:T(8,128)(2,1)S(1)}, f32[256,256]{1,0:T(8,128)S(1)}) custom-call(s32[2]{0:T(128)S(1)} %copy-done.5, s32[2,8]{1,0:T(2,128)S(1)} %copy-done.4, bf16[256,256]{1,0:T(8,128)(2,1)S(1)} %bitcast.4, bf16[2,8,128,128]{3,2,1,0:T(8,128)(2,1)S(1)} %copy-done, bf16[256,256]{1,0:T(8,128)(2,1)S(1)} %bitcast.5, ...), custom_call_target="tpu_custom_call" | custom-call | tf_op jit(solution)/shard_map/layer/pallas_call | solution.py:318
  29.1 0.0 copy-start.6
  29.1 0.7 %broadcast_maximum_fusion = bf16[256,256]{1,0:T(8,128)(2,1)} fusion(bf16[256,256]{1,0:T(8,128)(2,1)S(1)} %get-tuple-element.6), kind=kLoop, calls=%fused_computation.1 | loop fusion | flops 65536 | bytes 262144 | tf_op jit(solution)/shard_map/max | solution.py:333
  29.7 0.3 %copy-done.6 = s32[2,128,256]{2,1,0:T(8,128)S(1)} copy-done((s32[2,128,256]{2,1,0:T(8,128)S(1)}, s32[2,128,256]{2,1,0:T(8,128)}, u32[]{:S(2)}) %copy-start.6) | copy-done | bytes 262168
  30.1 0.7 %compare_select_fusion = bf16[2,128,256]{2,1,0:T(8,128)(2,1)} fusion(bf16[2,128,256]{2,1,0:T(8,128)(2,1)S(1)} %bitcast.6, s32[2,128,256]{2,1,0:T(8,128)S(1)} %copy-done.6), kind=kLoop, calls=%fused_computation | loop fusion | flops 131072 | bytes 524288 | tf_op jit(solution)/shard_map/jit(_where)/select_n | solution.py:334
  30.8 0.7 %copy.11 = f32[256,256]{1,0:T(8,128)} copy(f32[256,256]{1,0:T(8,128)S(1)} %get-tuple-element.13) | data formatting | bytes 524288
Async XLA Ops:
  0.6 0.7 %copy-start.4 = (s32[2,8]{1,0:T(2,128)S(1)}, s32[2,8]{1,0:T(2,128)}, u32[]{:S(2)}) copy-start(s32[2,8]{1,0:T(2,128)} %refs_1_.1) | copy-start | bytes 196
  0.6 0.7 %copy-start.5 = (s32[2]{0:T(128)S(1)}, s32[2]{0:T(128)}, u32[]{:S(2)}) copy-start(s32[2]{0:T(128)} %refs_0_.1) | copy-start | bytes 28
  1.3 1.0 %copy-start = (bf16[2,8,128,128]{3,2,1,0:T(8,128)(2,1)S(1)}, bf16[2,8,128,128]{3,2,1,0:T(8,128)(2,1)}, u32[]{:S(2)}) copy-start(bf16[2,8,128,128]{3,2,1,0:T(8,128)(2,1)} %refs_3_.1) | copy-start | bytes 1572868
  2.4 0.9 %copy-start.1 = (bf16[2,128,256]{2,1,0:T(8,128)(2,1)S(1)}, bf16[2,128,256]{2,1,0:T(8,128)(2,1)}, u32[]{:S(2)}) copy-start(bf16[2,128,256]{2,1,0:T(8,128)(2,1)} %param.7) | copy-start | bytes 393220
  3.3 0.9 %copy-start.2 = (bf16[2,128,256]{2,1,0:T(8,128)(2,1)S(1)}, bf16[2,128,256]{2,1,0:T(8,128)(2,1)}, u32[]{:S(2)}) copy-start(bf16[2,128,256]{2,1,0:T(8,128)(2,1)} %param.12) | copy-start | bytes 393220
  4.2 0.9 %copy-start.3 = (bf16[256,256]{1,0:T(8,128)(2,1)S(1)}, bf16[256,256]{1,0:T(8,128)(2,1)}, u32[]{:S(2)}) copy-start(bf16[256,256]{1,0:T(8,128)(2,1)} %refs_5_.1) | copy-start | bytes 393220
  29.1 1.0 %copy-start.6 = (s32[2,128,256]{2,1,0:T(8,128)S(1)}, s32[2,128,256]{2,1,0:T(8,128)}, u32[]{:S(2)}) copy-start(s32[2,128,256]{2,1,0:T(8,128)} %param.13) | copy-start | bytes 786436

commit v2 on v1

--- a/solution.py
+++ b/solution.py
@@ -27,12 +27,12 @@
 
 def kernel(dims, *refs):
     blk_size, rep_size, rows_per, slots, tile, width, plane_y, reduce_in = dims
-    (count_ref, cols_ref, feat_ref, tv_ref, grad_ref, weight_ref) = refs[:6]
-    (act_ref, col_ref, wg_ref) = refs[6:9]
-    (tv, grad, weight, feats, mt, rg, own, one_send, one_recv, two_send, two_recv,
+    (count_hbm, cols_hbm, feat_ref, tv_ref, grad_ref, weight_ref, mask_ref) = refs[:7]
+    (act_ref, col_ref, wg_ref) = refs[7:10]
+    (count_ref, cols_ref, mask, tv, grad, weight, feats, mt, rg, own, one_send, one_recv, two_send, two_recv,
      act, col, wg_part, rs_recv, z_buf, wg_full,
-     in_sem, out_sem, f_send, f_recv, fwd_send, one_ssem, one_rsem, two_ssem, two_rsem,
-     rs_ssem, rs_rsem, z_ssem, z_rsem, ag_ssem, ag_rsem) = refs[9:]
+     in_sem, f_send, f_recv, fwd_send, one_ssem, one_rsem, two_ssem, two_rsem,
+     rs_ssem, rs_rsem, z_ssem, z_rsem, ag_ssem, ag_rsem) = refs[10:]
     nodes = rows_per * tile
     chips = blk_size // 2
     z_size = rep_size // plane_y
@@ -61,6 +61,9 @@
     my_rows = pl.ds(pl.multiple_of(core * nodes, nodes), nodes)
     sib_rows = pl.ds(pl.multiple_of((1 - core) * nodes, nodes), nodes)
     loads.append(pltpu.make_async_copy(feat_ref, feats.at[chip, my_rows], in_sem.at[2 + rows_per]))
+    loads.append(pltpu.make_async_copy(count_hbm, count_ref, in_sem.at[3 + rows_per]))
+    loads.append(pltpu.make_async_copy(cols_hbm, cols_ref, in_sem.at[4 + rows_per]))
+    loads.append(pltpu.make_async_copy(mask_ref, mask, in_sem.at[5 + rows_per]))
     for load in loads:
         load.start()
 
@@ -113,10 +116,12 @@
 
     for piece in range(rows_per):
         each(chips - 1, lambda step: send_x(step, piece).start())
-    loads[-1].wait()
+    loads[2 + rows_per].wait()
     for piece in range(rows_per):
         pass_on(chip, piece).start()
 
+    loads[3 + rows_per].wait()
+    loads[4 + rows_per].wait()
     for t in range(rows_per):
         loads[2 + t].wait()
         tv[t, slots] = jnp.zeros((tile, tile), BF16)
@@ -176,7 +181,6 @@
             came_x(q, piece).wait_recv()
             pass_on(q, piece).start()
 
-    each(chips - 1, second)
     each(chips - 1, hand_on)
 
     for piece in range(rows_per):
@@ -210,8 +214,9 @@
             rs_copy(step).start()
     else:
         wg_ref[...] = term
-
-    act_ref[...] = dot(hidden, weight[...]).astype(BF16)
+    each(chips - 1, second)
+
+    act_ref[...] = jnp.maximum(dot(hidden, weight[...]), 0.0).astype(BF16)
     one_copy(chip).wait_recv()
     col[...] = own[chip] + one_recv[chip].astype(F32)
 
@@ -221,7 +226,8 @@
         col[...] += two_recv[q].astype(F32)
 
     each(chips - 1, gathered)
-    col_ref[...] = col[...].astype(BF16)
+    loads[5 + rows_per].wait()
+    col_ref[...] = (mask[...].astype(F32) * col[...]).astype(BF16)
 
     if reduce_in:
         my_share = pl.ds(pl.multiple_of(place * share, share), share)
@@ -271,6 +277,15 @@
             ag_copy(step, place).wait_send()
         for step in range(1, z_size):
             z_copy(step, my_z).wait_send()
+
+
+def write_out(a_ref, b_ref, c_ref, a_out, b_out, c_out, sem):
+    copies = [pltpu.make_async_copy(src, dst, sem.at[i])
+              for i, (src, dst) in enumerate(((a_ref, a_out), (b_ref, b_out), (c_ref, c_out)))]
+    for copy in copies:
+        copy.start()
+    for copy in copies:
+        copy.wait()
 
 
 def per_device(features, weight, tile_values, tile_count, tile_cols, out_grad, relu_mask):
@@ -288,6 +303,9 @@
     dma = pltpu.SemaphoreType.DMA
     vmem = pltpu.VMEM
     scratch = [
+        pltpu.SMEM((rows_per,), jnp.int32),
+        pltpu.SMEM((rows_per, slots), jnp.int32),
+        vmem(block, jnp.int32),
         vmem((rows_per, slots + 1, tile, tile), BF16),
         vmem(block, BF16),
         vmem((width, width), BF16),
@@ -305,33 +323,41 @@
         vmem((plane - 1, share, width), BF16),
         vmem((z_size, share, width), BF16),
         vmem((width, width), BF16),
-        dma((3 + rows_per,)), dma((2,)),
+        dma((6 + rows_per,)),
         dma((chips, rows_per)), dma((2, chips, rows_per)), dma((chips, rows_per)),
         dma((chips,)), dma((chips,)), dma((chips,)), dma((chips,)),
         dma((plane - 1,)), dma((plane - 1,)), dma((z_size,)), dma((z_size,)),
         dma((plane - 1,)), dma((plane - 1,)),
     ]
-    smem = pl.BlockSpec(memory_space=pltpu.SMEM)
-    hbm = pl.BlockSpec(memory_space=pl.ANY)
+    hbm = pl.BlockSpec(memory_space=pltpu.HBM)
     whole = pl.BlockSpec(memory_space=pltpu.VMEM)
     dims = (blk_size, rep_size, rows_per, slots, tile, width, plane_y, reduce_in)
-    linear, column, weight_term = pl.pallas_call(
+    results = pl.pallas_call(
         functools.partial(kernel, dims),
         out_shape=(
             jax.ShapeDtypeStruct(block, BF16),
             jax.ShapeDtypeStruct(block, BF16),
             jax.ShapeDtypeStruct((width, width), F32),
         ),
-        in_specs=[smem, smem, hbm, hbm, hbm, hbm],
+        in_specs=[hbm] * 7,
         out_specs=(whole, whole, whole),
         scratch_shapes=scratch,
         compiler_params=pltpu.CompilerParams(
             collective_id=0, has_side_effects=True, vmem_limit_bytes=32 * 1024 * 1024
         ),
         name="layer",
-    )(tile_count, tile_cols, features.reshape(block), tile_values, out_grad.reshape(block), weight)
-    activated = jnp.maximum(linear, 0).reshape(features.shape)
-    in_grad = jnp.where(relu_mask != 0, column.reshape(features.shape), jnp.zeros((), BF16))
+    )(*[pltpu.with_memory_space_constraint(x, pltpu.HBM) for x in (
+        tile_count, tile_cols, features.reshape(block), tile_values, out_grad.reshape(block), weight,
+        relu_mask.reshape(block))])
+    activated, in_grad, weight_term = pl.pallas_call(
+        write_out,
+        out_shape=tuple(jax.ShapeDtypeStruct(r.shape, r.dtype) for r in results),
+        in_specs=[whole] * 3,
+        out_specs=(hbm, hbm, hbm),
+        scratch_shapes=[dma((3,))],
+        name="write_out",
+    )(*results)
+    activated, in_grad = activated.reshape(features.shape), in_grad.reshape(features.shape)
     if not reduce_in:
         scale = 1.0 / math.sqrt(nodes * blk_size * rep_size)
         weight_term = lax.psum(weight_term, ("blk", "rep")) * scale

time: 31.7 us -> 29.9 us (0.943)
  local copies, waits for them, and re-layouts: 5.45 us -> 2 us
  Pallas kernels: 24 us -> 27.1 us
  other arithmetic: 1.36 us -> 0 us
    unnamed x15 -> x6, local copies, waits for them, and re-layouts: 5.45 us -> 2 us
    pallas_call x0 -> x1, Pallas kernels: none -> 1.9 us  [per_device(): pl.pallas_call(write_out, out_shape=tuple((jax.ShapeDtypeStruct(r.shape,...]
    pallas_call x1, Pallas kernels: 24 us -> 25.2 us  [per_device(): pl.pallas_call(functools.partial(kernel, dims), out_shape=(jax.ShapeDtype...]
    select_n x1 -> x0, other arithmetic: 0.69 us -> none  [per_device(): jnp.where(relu_mask != 0, column.reshape(features.shape), jnp.zeros((), B...]
    max x1 -> x0, other arithmetic: 0.67 us -> none  [per_device(): activated = jnp.maximum(linear, 0).reshape(features.shape)]
where the time goes in v2:
time: 29.9 us; the launch traced here: 29.7 us
  Pallas kernels  27.1 us (91%)
  local copies, waits for them, and re-layouts  2 us (7%)
  between operations  0.65 us (2%)
    pallas_call x1, Pallas kernels, per_device(): pl.pallas_call(functools.partial(kernel, dims), out_shape=(jax.ShapeDtype...  25.2 us
    unnamed x6, local copies, waits for them, and re-layouts  2 us
    pallas_call x1, Pallas kernels, per_device(): pl.pallas_call(write_out, out_shape=tuple((jax.ShapeDtypeStruct(r.shape,...  1.9 us

profile of v2, /device:TPU:0, one launch (start us, length us, event | category | flops | bytes accessed | tf_op | source)
XLA Modules:
  0.0 29.7 jit_solution(14663360230921436017)
XLA Ops:
  0.6 25.2 %layer.1 = (bf16[256,256]{1,0:T(8,128)(2,1)S(1)}, bf16[256,256]{1,0:T(8,128)(2,1)S(1)}, f32[256,256]{1,0:T(8,128)S(1)}) custom-call(s32[2]{0:T(128)} %refs_0_.1, s32[2,8]{1,0:T(2,128)} %refs_1_.1, bf16[256,256]{1,0:T(8,128)(2,1)} %bitcast.6, bf16[2,8,128,128]{3,2,1,0:T(8,128)(2,1)} %refs_3_.1, bf16[256,256]{1,0:T(8,128)(2,1)} %bitcast.7, ...), custom_call_target="tpu_custom_call" | custom-call | tf_op jit(solution)/shard_map/layer/pallas_call | solution.py:335
  25.8 0.0 copy-start
  25.8 0.7 %copy-done = f32[256,256]{1,0:T(8,128)} copy-done((f32[256,256]{1,0:T(8,128)}, f32[256,256]{1,0:T(8,128)S(1)}, u32[]{:S(2)}) %copy-start) | copy-done | bytes 262168
  26.5 0.0 copy-start.1
  26.5 0.6 %copy-done.1 = bf16[256,256]{1,0:T(8,128)(2,1)} copy-done((bf16[256,256]{1,0:T(8,128)(2,1)}, bf16[256,256]{1,0:T(8,128)(2,1)S(1)}, u32[]{:S(2)}) %copy-start.1) | copy-done | bytes 131096
  27.2 0.0 copy-start.2
  27.2 0.7 %copy-done.2 = bf16[256,256]{1,0:T(8,128)(2,1)} copy-done((bf16[256,256]{1,0:T(8,128)(2,1)}, bf16[256,256]{1,0:T(8,128)(2,1)S(1)}, u32[]{:S(2)}) %copy-start.2) | copy-done | bytes 131096
  27.8 1.9 %write_out.1 = (bf16[256,256]{1,0:T(8,128)(2,1)}, bf16[256,256]{1,0:T(8,128)(2,1)}, f32[256,256]{1,0:T(8,128)}) custom-call(bf16[256,256]{1,0:T(8,128)(2,1)} %copy-done.1, bf16[256,256]{1,0:T(8,128)(2,1)} %copy-done.2, f32[256,256]{1,0:T(8,128)} %copy-done), custom_call_target="tpu_custom_call" | custom-call | tf_op jit(solution)/shard_map/write_out/pallas_call | solution.py:352
Async XLA Ops:
  25.8 0.7 %copy-start = (f32[256,256]{1,0:T(8,128)}, f32[256,256]{1,0:T(8,128)S(1)}, u32[]{:S(2)}) copy-start(f32[256,256]{1,0:T(8,128)S(1)} %get-tuple-element.11.c_ref) | copy-start | bytes 786436
  26.5 0.6 %copy-start.1 = (bf16[256,256]{1,0:T(8,128)(2,1)}, bf16[256,256]{1,0:T(8,128)(2,1)S(1)}, u32[]{:S(2)}) copy-start(bf16[256,256]{1,0:T(8,128)(2,1)S(1)} %get-tuple-element.9.a_ref) | copy-start | bytes 393220
  27.2 0.7 %copy-start.2 = (bf16[256,256]{1,0:T(8,128)(2,1)}, bf16[256,256]{1,0:T(8,128)(2,1)S(1)}, u32[]{:S(2)}) copy-start(bf16[256,256]{1,0:T(8,128)(2,1)S(1)} %get-tuple-element.10.b_ref) | copy-start | bytes 393220

commit v3 on v2

--- a/solution.py
+++ b/solution.py
@@ -29,8 +29,8 @@
     blk_size, rep_size, rows_per, slots, tile, width, plane_y, reduce_in = dims
     (count_hbm, cols_hbm, feat_ref, tv_ref, grad_ref, weight_ref, mask_ref) = refs[:7]
     (act_ref, col_ref, wg_ref) = refs[7:10]
-    (count_ref, cols_ref, mask, tv, grad, weight, feats, mt, rg, own, one_send, one_recv, two_send, two_recv,
-     act, col, wg_part, rs_recv, z_buf, wg_full,
+    (count_ref, cols_ref, mask, tv, grad, weight, feats, dense, own, one_send, one_recv, two_send, two_recv,
+     act, col, term, wg_part, rs_recv, z_buf, wg_full,
      in_sem, f_send, f_recv, fwd_send, one_ssem, one_rsem, two_ssem, two_rsem,
      rs_ssem, rs_rsem, z_ssem, z_rsem, ag_ssem, ag_rsem) = refs[10:]
     nodes = rows_per * tile
@@ -53,6 +53,20 @@
     def z_id(step):
         there = lax.rem(my_z + step, z_size)
         return there, {"blk": blk, "rep": there * plane_y + my_y}
+
+    barrier = pltpu.get_barrier_semaphore()
+    if reduce_in:
+        for step in range(1, plane):
+            pl.semaphore_signal(barrier, inc=1, device_id=plane_id(step)[1], device_id_type=MESH)
+        for step in range(1, z_size):
+            pl.semaphore_signal(barrier, inc=1, device_id=z_id(step)[1], device_id_type=MESH)
+        greeted = plane - 1 + z_size - 1
+    else:
+        pl.semaphore_signal(barrier, inc=1, device_id={"blk": sib, "rep": rep}, device_id_type=MESH)
+        for step in range(chips - 1):
+            pl.semaphore_signal(
+                barrier, inc=1, device_id={"blk": other_chip(step) * 2 + core, "rep": rep}, device_id_type=MESH)
+        greeted = chips
 
     loads = [pltpu.make_async_copy(grad_ref, grad, in_sem.at[0]),
              pltpu.make_async_copy(weight_ref, weight, in_sem.at[1])]
@@ -66,23 +80,6 @@
     loads.append(pltpu.make_async_copy(mask_ref, mask, in_sem.at[5 + rows_per]))
     for load in loads:
         load.start()
-
-    barrier = pltpu.get_barrier_semaphore()
-    if reduce_in:
-        for step in range(1, plane):
-            pl.semaphore_signal(barrier, inc=1, device_id=plane_id(step)[1], device_id_type=MESH)
-        for step in range(1, z_size):
-            pl.semaphore_signal(barrier, inc=1, device_id=z_id(step)[1], device_id_type=MESH)
-        greeted = plane - 1 + z_size - 1
-    else:
-        pl.semaphore_signal(barrier, inc=1, device_id={"blk": sib, "rep": rep}, device_id_type=MESH)
-        for step in range(chips - 1):
-            pl.semaphore_signal(
-                barrier, inc=1, device_id={"blk": other_chip(step) * 2 + core, "rep": rep}, device_id_type=MESH)
-        greeted = chips
-    loads[0].wait()
-    loads[1].wait()
-    rg[...] = dot(grad[...], weight[...], ((1,), (1,))).astype(BF16)
     pl.semaphore_wait(barrier, greeted)
 
     def send_x(step, piece):
@@ -122,9 +119,12 @@
 
     loads[3 + rows_per].wait()
     loads[4 + rows_per].wait()
+    loads[0].wait()
     for t in range(rows_per):
         loads[2 + t].wait()
         tv[t, slots] = jnp.zeros((tile, tile), BF16)
+
+    used = [[jnp.where(s < count_ref[t], cols_ref[t, s], -1) for s in range(slots)] for t in range(rows_per)]
 
     def block_of(q, c):
         member = q * 2 + c
@@ -135,8 +135,7 @@
             for t in range(rows_per):
                 slot = jnp.int32(slots)
                 for s in range(slots):
-                    hit = jnp.logical_and(cols_ref[t, s] == column, s < count_ref[t])
-                    slot = jnp.where(hit, jnp.int32(s), slot)
+                    slot = jnp.where(used[t][s] == column, jnp.int32(s), slot)
                 pieces.append(tv[t, slot])
             bands.append(jnp.concatenate(pieces, axis=1))
         return jnp.concatenate(bands, axis=0)
@@ -156,51 +155,77 @@
     def for_sibling(step):
         q = other_chip(step)
         block = block_of(q, 1 - core)
-        one_send[q] = dot(block, rg[...]).astype(BF16)
+        one_send[q] = dot(block, grad[...]).astype(BF16)
         one_copy(q).start()
-        mt[q, :, sib_rows] = block.T
+        dense[q, sib_rows] = block
 
     def for_core(step):
         q = other_chip(step)
         block = block_of(q, core)
-        own[q] = dot(block, rg[...])
-        mt[q, :, my_rows] = block.T
+        own[q] = dot(block, grad[...])
+        dense[q, my_rows] = block
+
+    def pair(step):
+        q = other_chip(step)
+        one_copy(q).wait_recv()
+        total = own[q] + one_recv[q].astype(F32)
+        own[q] = total
+        two_send[q] = total.astype(BF16)
 
     each(chips, for_sibling)
     each(chips, for_core)
-
-    def second(step):
-        q = other_chip(step)
-        one_copy(q).wait_recv()
-        two_send[q] = (own[q] + one_recv[q].astype(F32)).astype(BF16)
-        two_copy(q, chip).start()
-
-    def hand_on(step):
+    each(chips, pair)
+
+    term[...] = dot(feats[chip, my_rows], two_send[chip], ((0,), (0,)))
+
+    def arrive(step):
         q = other_chip(step)
         for piece in range(rows_per):
             came_x(q, piece).wait_recv()
             pass_on(q, piece).start()
-
-    each(chips - 1, hand_on)
-
-    for piece in range(rows_per):
-        passed(chip, piece).wait_recv()
-    own_part = dot(mt[chip], feats[chip])
-    act[...] = own_part
-
-    def forward(step):
-        q = other_chip(step)
+        term[...] += dot(feats[q, my_rows], two_send[q], ((0,), (0,)))
+
+    each(chips - 1, arrive)
+
+    def forward():
         for piece in range(rows_per):
-            passed(q, piece).wait_recv()
-        act[...] += dot(mt[q], feats[q])
-
-    each(chips - 1, forward)
-    hidden = act[...].astype(BF16)
-    term = dot(hidden, grad[...], ((0,), (0,)))
+            passed(chip, piece).wait_recv()
+        act[...] = dot(dense[chip], feats[chip], ((0,), (0,)))
+
+        def from_chip(step):
+            q = other_chip(step)
+            for piece in range(rows_per):
+                passed(q, piece).wait_recv()
+            act[...] += dot(dense[q], feats[q], ((0,), (0,)))
+
+        each(chips - 1, from_chip)
+
+    def activate():
+        loads[1].wait()
+        act_ref[...] = jnp.maximum(dot(act[...].astype(BF16), weight[...]), 0.0).astype(BF16)
+
+    def columns():
+        col[...] = own[chip]
+
+        def from_chip(step):
+            q = other_chip(step)
+            two_copy(q, q).wait_recv()
+            col[...] += two_recv[q].astype(F32)
+
+        each(chips - 1, from_chip)
+        high = col[...].astype(BF16)
+        low = (col[...] - high.astype(F32)).astype(BF16)
+        back = dot(high, weight[...], ((1,), (1,))) + dot(low, weight[...], ((1,), (1,)))
+        loads[5 + rows_per].wait()
+        col_ref[...] = (mask[...].astype(F32) * back).astype(BF16)
+
+    def second(step):
+        q = other_chip(step)
+        two_copy(q, chip).start()
 
     if reduce_in:
         share = width // plane
-        wg_part[...] = term.astype(BF16)
+        wg_part[...] = term[...].astype(BF16)
 
         def rs_copy(step):
             there, device = plane_id(step)
@@ -212,26 +237,10 @@
 
         for step in range(1, plane):
             rs_copy(step).start()
-    else:
-        wg_ref[...] = term
-    each(chips - 1, second)
-
-    act_ref[...] = jnp.maximum(dot(hidden, weight[...]), 0.0).astype(BF16)
-    one_copy(chip).wait_recv()
-    col[...] = own[chip] + one_recv[chip].astype(F32)
-
-    def gathered(step):
-        q = other_chip(step)
-        two_copy(q, q).wait_recv()
-        col[...] += two_recv[q].astype(F32)
-
-    each(chips - 1, gathered)
-    loads[5 + rows_per].wait()
-    col_ref[...] = (mask[...].astype(F32) * col[...]).astype(BF16)
-
-    if reduce_in:
+        each(chips - 1, second)
+        forward()
         my_share = pl.ds(pl.multiple_of(place * share, share), share)
-        total = wg_part[my_share].astype(F32)
+        total = term[my_share]
         for step in range(1, plane):
             rs_copy(step).wait_recv()
             total = total + rs_recv[step - 1].astype(F32)
@@ -245,6 +254,7 @@
 
         for step in range(1, z_size):
             z_copy(step, my_z).start()
+        activate()
         for step in range(1, z_size):
             z_copy(step, z_id(step)[0]).wait_recv()
         total = z_buf[0].astype(F32)
@@ -262,9 +272,16 @@
 
         for step in range(1, plane):
             ag_copy(step, place).start()
+        columns()
         for step in range(1, plane):
             ag_copy(step, lax.rem(place + plane - step, plane)).wait_recv()
         wg_ref[...] = wg_full[...].astype(F32)
+    else:
+        wg_ref[...] = term[...]
+        each(chips - 1, second)
+        forward()
+        activate()
+        columns()
 
     for piece in range(rows_per):
         each(chips - 1, lambda step: send_x(step, piece).wait_send())
@@ -310,8 +327,7 @@
         vmem(block, BF16),
         vmem((width, width), BF16),
         vmem((chips, 2 * nodes, width), BF16),
-        vmem((chips, nodes, 2 * nodes), BF16),
-        vmem(block, BF16),
+        vmem((chips, 2 * nodes, nodes), BF16),
         vmem((chips,) + block, F32),
         vmem((chips,) + block, BF16),
         vmem((chips,) + block, BF16),
@@ -319,6 +335,7 @@
         vmem((chips,) + block, BF16),
         vmem(block, F32),
         vmem(block, F32),
+        vmem((width, width), F32),
         vmem((width, width), BF16),
         vmem((plane - 1, share, width), BF16),
         vmem((z_size, share, width), BF16),
@@ -355,6 +372,7 @@
         in_specs=[whole] * 3,
         out_specs=(hbm, hbm, hbm),
         scratch_shapes=[dma((3,))],
+        compiler_params=pltpu.CompilerParams(vmem_limit_bytes=4 * 1024 * 1024),
         name="write_out",
     )(*results)
     activated, in_grad = activated.reshape(features.shape), in_grad.reshape(features.shape)

time: 29.9 us -> 23.7 us (0.79)
  Pallas kernels: 27.1 us -> 22.9 us
  local copies, waits for them, and re-layouts: 2 us -> 0 us
    pallas_call x1, Pallas kernels: 25.2 us -> 22.1 us  [per_device(): pl.pallas_call(functools.partial(kernel, dims), out_shape=(jax.ShapeDtype...]
    unnamed x6 -> x0, local copies, waits for them, and re-layouts: 2 us -> none
    pallas_call x1, Pallas kernels: 1.9 us -> 0.82 us  [per_device(): pl.pallas_call(write_out, out_shape=tuple((jax.ShapeDtypeStruct(r.shape,...]
where the time goes in v3:
time: 23.7 us; the launch traced here: 23.5 us
  Pallas kernels  22.9 us (97%)
  between operations  0.64 us (3%)
    pallas_call x1, Pallas kernels, per_device(): pl.pallas_call(functools.partial(kernel, dims), out_shape=(jax.ShapeDtype...  22.1 us
    pallas_call x1, Pallas kernels, per_device(): pl.pallas_call(write_out, out_shape=tuple((jax.ShapeDtypeStruct(r.shape,...  0.82 us

profile of v3, /device:TPU:0, one launch (start us, length us, event | category | flops | bytes accessed | tf_op | source)
XLA Modules:
  0.0 23.5 jit_solution(16413978771522021890)
XLA Ops:
  0.6 22.1 %layer.1 = (bf16[256,256]{1,0:T(8,128)(2,1)S(1)}, bf16[256,256]{1,0:T(8,128)(2,1)S(1)}, f32[256,256]{1,0:T(8,128)S(1)}) custom-call(s32[2]{0:T(128)} %refs_0_.1, s32[2,8]{1,0:T(2,128)} %refs_1_.1, bf16[256,256]{1,0:T(8,128)(2,1)} %bitcast.6, bf16[2,8,128,128]{3,2,1,0:T(8,128)(2,1)} %refs_3_.1, bf16[256,256]{1,0:T(8,128)(2,1)} %bitcast.7, ...), custom_call_target="tpu_custom_call" | custom-call | tf_op jit(solution)/shard_map/layer/pallas_call | solution.py:352
  22.7 0.8 %write_out.1 = (bf16[256,256]{1,0:T(8,128)(2,1)}, bf16[256,256]{1,0:T(8,128)(2,1)}, f32[256,256]{1,0:T(8,128)}) custom-call(bf16[256,256]{1,0:T(8,128)(2,1)S(1)} %get-tuple-element.9.a_ref, bf16[256,256]{1,0:T(8,128)(2,1)S(1)} %get-tuple-element.10.b_ref, f32[256,256]{1,0:T(8,128)S(1)} %get-tuple-element.11.c_ref), custom_call_target="tpu_custom_call" | custom-call | tf_op jit(solution)/shard_map/write_out/pallas_call | solution.py:369

commit v4 on v3

--- a/solution.py
+++ b/solution.py
@@ -33,7 +33,7 @@
      act, col, term, wg_part, rs_recv, z_buf, wg_full,
      in_sem, f_send, f_recv, fwd_send, one_ssem, one_rsem, two_ssem, two_rsem,
      rs_ssem, rs_rsem, z_ssem, z_rsem, ag_ssem, ag_rsem) = refs[10:]
-    nodes = rows_per * tile
+    nodes, half = rows_per * tile, width // 2
     chips = blk_size // 2
     z_size = rep_size // plane_y
     plane = blk_size * plane_y
@@ -78,43 +78,42 @@
     loads.append(pltpu.make_async_copy(count_hbm, count_ref, in_sem.at[3 + rows_per]))
     loads.append(pltpu.make_async_copy(cols_hbm, cols_ref, in_sem.at[4 + rows_per]))
     loads.append(pltpu.make_async_copy(mask_ref, mask, in_sem.at[5 + rows_per]))
-    for load in loads:
-        load.start()
+    for i in [3 + rows_per, 4 + rows_per] + list(range(2, 2 + rows_per)) + [0, 2 + rows_per]:
+        loads[i].start()
     pl.semaphore_wait(barrier, greeted)
 
+    def x_copy(origin, device, piece):
+        lanes = pl.ds(piece * half, half)
+        return pltpu.make_async_remote_copy(
+            src_ref=feat_ref.at[:, lanes], dst_ref=feats.at[origin, my_rows, lanes],
+            send_sem=f_send.at[device // 2, piece], recv_sem=f_recv.at[0, origin, piece],
+            device_id={"blk": device, "rep": rep}, device_id_type=MESH)
+
     def send_x(step, piece):
-        q = other_chip(step)
-        rows = pl.ds(pl.multiple_of(core * nodes + piece * tile, tile), tile)
+        return x_copy(chip, other_chip(step) * 2 + core, piece)
+
+    def came_x(q, piece):
+        return x_copy(q, q * 2 + core, piece)
+
+    def sib_copy(q, rows, piece):
+        lanes = pl.ds(piece * half, half)
         return pltpu.make_async_remote_copy(
-            src_ref=feat_ref.at[pl.ds(piece * tile, tile)], dst_ref=feats.at[chip, rows],
-            send_sem=f_send.at[q, piece], recv_sem=f_recv.at[0, chip, piece],
-            device_id={"blk": q * 2 + core, "rep": rep}, device_id_type=MESH)
-
-    def came_x(q, piece):
-        rows = pl.ds(pl.multiple_of(core * nodes + piece * tile, tile), tile)
-        return pltpu.make_async_remote_copy(
-            src_ref=feat_ref.at[pl.ds(piece * tile, tile)], dst_ref=feats.at[q, rows],
-            send_sem=f_send.at[q, piece], recv_sem=f_recv.at[0, q, piece],
-            device_id={"blk": q * 2 + core, "rep": rep}, device_id_type=MESH)
-
-    def pass_on(q, piece):
-        rows = pl.ds(pl.multiple_of(core * nodes + piece * tile, tile), tile)
-        return pltpu.make_async_remote_copy(
-            src_ref=feats.at[q, rows], dst_ref=feats.at[q, rows],
+            src_ref=feats.at[q, rows, lanes], dst_ref=feats.at[q, rows, lanes],
             send_sem=fwd_send.at[q, piece], recv_sem=f_recv.at[1, q, piece],
             device_id={"blk": sib, "rep": rep}, device_id_type=MESH)
 
+    def pass_on(q, piece):
+        return sib_copy(q, my_rows, piece)
+
     def passed(q, piece):
-        rows = pl.ds(pl.multiple_of((1 - core) * nodes + piece * tile, tile), tile)
-        return pltpu.make_async_remote_copy(
-            src_ref=feats.at[q, rows], dst_ref=feats.at[q, rows],
-            send_sem=fwd_send.at[q, piece], recv_sem=f_recv.at[1, q, piece],
-            device_id={"blk": sib, "rep": rep}, device_id_type=MESH)
-
-    for piece in range(rows_per):
+        return sib_copy(q, sib_rows, piece)
+
+    for piece in range(2):
         each(chips - 1, lambda step: send_x(step, piece).start())
+    loads[1].start()
+    loads[5 + rows_per].start()
     loads[2 + rows_per].wait()
-    for piece in range(rows_per):
+    for piece in range(2):
         pass_on(chip, piece).start()
 
     loads[3 + rows_per].wait()
@@ -178,23 +177,25 @@
 
     term[...] = dot(feats[chip, my_rows], two_send[chip], ((0,), (0,)))
 
-    def arrive(step):
-        q = other_chip(step)
-        for piece in range(rows_per):
+    def arrive(piece):
+        rows = pl.ds(piece * half, half)
+
+        def from_chip(step):
+            q = other_chip(step)
             came_x(q, piece).wait_recv()
             pass_on(q, piece).start()
-        term[...] += dot(feats[q, my_rows], two_send[q], ((0,), (0,)))
-
-    each(chips - 1, arrive)
+            term[rows] += dot(feats[q, my_rows, rows], two_send[q], ((0,), (0,)))
+
+        each(chips - 1, from_chip)
 
     def forward():
-        for piece in range(rows_per):
+        for piece in range(2):
             passed(chip, piece).wait_recv()
         act[...] = dot(dense[chip], feats[chip], ((0,), (0,)))
 
         def from_chip(step):
             q = other_chip(step)
-            for piece in range(rows_per):
+            for piece in range(2):
                 passed(q, piece).wait_recv()
             act[...] += dot(dense[q], feats[q], ((0,), (0,)))
 
@@ -224,76 +225,86 @@
         two_copy(q, chip).start()
 
     if reduce_in:
-        share = width // plane
-        wg_part[...] = term[...].astype(BF16)
-
-        def rs_copy(step):
+        share = half // plane
+        scale = 1.0 / math.sqrt(nodes * blk_size * rep_size)
+
+        def rows_of(piece, owner):
+            return pl.ds(pl.multiple_of(piece * half + owner * share, share), share)
+
+        def rs_copy(piece, step):
             there, device = plane_id(step)
             return pltpu.make_async_remote_copy(
-                src_ref=wg_part.at[pl.ds(pl.multiple_of(there * share, share), share)],
-                dst_ref=rs_recv.at[step - 1],
-                send_sem=rs_ssem.at[step - 1], recv_sem=rs_rsem.at[step - 1],
+                src_ref=wg_part.at[rows_of(piece, there)], dst_ref=rs_recv.at[piece, step - 1],
+                send_sem=rs_ssem.at[piece, step - 1], recv_sem=rs_rsem.at[piece, step - 1],
                 device_id=device, device_id_type=MESH)
 
-        for step in range(1, plane):
-            rs_copy(step).start()
-        each(chips - 1, second)
-        forward()
-        my_share = pl.ds(pl.multiple_of(place * share, share), share)
-        total = term[my_share]
-        for step in range(1, plane):
-            rs_copy(step).wait_recv()
-            total = total + rs_recv[step - 1].astype(F32)
-        z_buf[my_z] = total.astype(BF16)
-
-        def z_copy(step, slot):
+        def z_copy(piece, step, slot):
             return pltpu.make_async_remote_copy(
-                src_ref=z_buf.at[my_z], dst_ref=z_buf.at[slot],
-                send_sem=z_ssem.at[step - 1], recv_sem=z_rsem.at[slot],
+                src_ref=z_buf.at[piece, my_z], dst_ref=z_buf.at[piece, slot],
+                send_sem=z_ssem.at[piece, step - 1], recv_sem=z_rsem.at[piece, slot],
                 device_id=z_id(step)[1], device_id_type=MESH)
 
-        for step in range(1, z_size):
-            z_copy(step, my_z).start()
-        activate()
-        for step in range(1, z_size):
-            z_copy(step, z_id(step)[0]).wait_recv()
-        total = z_buf[0].astype(F32)
-        for z in range(1, z_size):
-            total = total + z_buf[z].astype(F32)
-        scale = 1.0 / math.sqrt(nodes * blk_size * rep_size)
-        wg_full[my_share] = (total * scale).astype(BF16)
-
-        def ag_copy(step, owner):
-            rows = pl.ds(pl.multiple_of(owner * share, share), share)
+        def ag_copy(piece, step, owner):
+            rows = rows_of(piece, owner)
             return pltpu.make_async_remote_copy(
                 src_ref=wg_full.at[rows], dst_ref=wg_full.at[rows],
-                send_sem=ag_ssem.at[step - 1], recv_sem=ag_rsem.at[step - 1],
+                send_sem=ag_ssem.at[piece, step - 1], recv_sem=ag_rsem.at[piece, step - 1],
                 device_id=plane_id(step)[1], device_id_type=MESH)
 
-        for step in range(1, plane):
-            ag_copy(step, place).start()
+        for piece in range(2):
+            arrive(piece)
+            rows = pl.ds(piece * half, half)
+            wg_part[rows] = term[rows].astype(BF16)
+            for step in range(1, plane):
+                rs_copy(piece, step).start()
+        each(chips - 1, second)
+        for piece in range(2):
+            total = term[rows_of(piece, place)]
+            for step in range(1, plane):
+                rs_copy(piece, step).wait_recv()
+                total = total + rs_recv[piece, step - 1].astype(F32)
+            z_buf[piece, my_z] = total.astype(BF16)
+            for step in range(1, z_size):
+                z_copy(piece, step, my_z).start()
+        forward()
+        for piece in range(2):
+            for step in range(1, z_size):
+                z_copy(piece, step, z_id(step)[0]).wait_recv()
+            total = z_buf[piece, 0].astype(F32)
+            for z in range(1, z_size):
+                total = total + z_buf[piece, z].astype(F32)
+            wg_full[rows_of(piece, place)] = (total * scale).astype(BF16)
+            for step in range(1, plane):
+                ag_copy(piece, step, place).start()
+            if piece == 0:
+                activate()
         columns()
-        for step in range(1, plane):
-            ag_copy(step, lax.rem(place + plane - step, plane)).wait_recv()
-        wg_ref[...] = wg_full[...].astype(F32)
+        for piece in range(2):
+            for step in range(1, plane):
+                ag_copy(piece, step, lax.rem(place + plane - step, plane)).wait_recv()
+            rows = pl.ds(piece * half, half)
+            wg_ref[rows] = wg_full[rows].astype(F32)
     else:
+        for piece in range(2):
+            arrive(piece)
         wg_ref[...] = term[...]
         each(chips - 1, second)
         forward()
         activate()
         columns()
 
-    for piece in range(rows_per):
+    for piece in range(2):
         each(chips - 1, lambda step: send_x(step, piece).wait_send())
         each(chips, lambda step: pass_on(other_chip(step), piece).wait_send())
     each(chips, lambda step: one_copy(other_chip(step)).wait_send())
     each(chips - 1, lambda step: two_copy(other_chip(step), chip).wait_send())
     if reduce_in:
-        for step in range(1, plane):
-            rs_copy(step).wait_send()
-            ag_copy(step, place).wait_send()
-        for step in range(1, z_size):
-            z_copy(step, my_z).wait_send()
+        for piece in range(2):
+            for step in range(1, plane):
+                rs_copy(piece, step).wait_send()
+                ag_copy(piece, step, place).wait_send()
+            for step in range(1, z_size):
+                z_copy(piece, step, my_z).wait_send()
 
 
 def write_out(a_ref, b_ref, c_ref, a_out, b_out, c_out, sem):
@@ -314,8 +325,8 @@
     plane_y = 2
     z_size = rep_size // plane_y
     plane = blk_size * plane_y
-    reduce_in = width % (plane * 16) == 0 and z_size <= 8
-    share = width // plane if reduce_in else 16
+    reduce_in = width % (plane * 32) == 0 and z_size <= 8
+    share = width // 2 // plane if reduce_in else 16
     block = (nodes, width)
     dma = pltpu.SemaphoreType.DMA
     vmem = pltpu.VMEM
@@ -337,14 +348,14 @@
         vmem(block, F32),
         vmem((width, width), F32),
         vmem((width, width), BF16),
-        vmem((plane - 1, share, width), BF16),
-        vmem((z_size, share, width), BF16),
+        vmem((2, plane - 1, share, width), BF16),
+        vmem((2, z_size, share, width), BF16),
         vmem((width, width), BF16),
         dma((6 + rows_per,)),
-        dma((chips, rows_per)), dma((2, chips, rows_per)), dma((chips, rows_per)),
+        dma((chips, 2)), dma((2, chips, 2)), dma((chips, 2)),
         dma((chips,)), dma((chips,)), dma((chips,)), dma((chips,)),
-        dma((plane - 1,)), dma((plane - 1,)), dma((z_size,)), dma((z_size,)),
-        dma((plane - 1,)), dma((plane - 1,)),
+        dma((2, plane - 1)), dma((2, plane - 1)), dma((2, z_size)), dma((2, z_size)),
+        dma((2, plane - 1)), dma((2, plane - 1)),
     ]
     hbm = pl.BlockSpec(memory_space=pltpu.HBM)
     whole = pl.BlockSpec(memory_space=pltpu.VMEM)

time: 23.7 us -> 23.3 us (0.983)
  Pallas kernels: 22.9 us -> 22.5 us
    pallas_call x1, Pallas kernels: 22.1 us -> 21.7 us  [per_device(): pl.pallas_call(functools.partial(kernel, dims), out_shape=(jax.ShapeDtype...]
where the time goes in v4:
time: 23.3 us; the launch traced here: 23.1 us
  Pallas kernels  22.5 us (97%)
  between operations  0.64 us (3%)
    pallas_call x1, Pallas kernels, per_device(): pl.pallas_call(functools.partial(kernel, dims), out_shape=(jax.ShapeDtype...  21.7 us
    pallas_call x1, Pallas kernels, per_device(): pl.pallas_call(write_out, out_shape=tuple((jax.ShapeDtypeStruct(r.shape,...  0.82 us

profile of v4, /device:TPU:0, one launch (start us, length us, event | category | flops | bytes accessed | tf_op | source)
XLA Modules:
  0.0 23.1 jit_solution(17780535736816416461)
XLA Ops:
  0.6 21.7 %layer.1 = (bf16[256,256]{1,0:T(8,128)(2,1)S(1)}, bf16[256,256]{1,0:T(8,128)(2,1)S(1)}, f32[256,256]{1,0:T(8,128)S(1)}) custom-call(s32[2]{0:T(128)} %refs_0_.1, s32[2,8]{1,0:T(2,128)} %refs_1_.1, bf16[256,256]{1,0:T(8,128)(2,1)} %bitcast.6, bf16[2,8,128,128]{3,2,1,0:T(8,128)(2,1)} %refs_3_.1, bf16[256,256]{1,0:T(8,128)(2,1)} %bitcast.7, ...), custom_call_target="tpu_custom_call" | custom-call | tf_op jit(solution)/shard_map/layer/pallas_call | solution.py:363
  22.3 0.8 %write_out.1 = (bf16[256,256]{1,0:T(8,128)(2,1)}, bf16[256,256]{1,0:T(8,128)(2,1)}, f32[256,256]{1,0:T(8,128)}) custom-call(bf16[256,256]{1,0:T(8,128)(2,1)S(1)} %get-tuple-element.9.a_ref, bf16[256,256]{1,0:T(8,128)(2,1)S(1)} %get-tuple-element.10.b_ref, f32[256,256]{1,0:T(8,128)S(1)} %get-tuple-element.11.c_ref), custom_call_target="tpu_custom_call" | custom-call | tf_op jit(solution)/shard_map/write_out/pallas_call | solution.py:380

commit v5 on v4

--- a/solution.py
+++ b/solution.py
@@ -56,7 +56,7 @@
 
     barrier = pltpu.get_barrier_semaphore()
     if reduce_in:
-        for step in range(1, plane):
+        for step in sorted(range(1, plane), key=lambda s: min(s, plane - s)):
             pl.semaphore_signal(barrier, inc=1, device_id=plane_id(step)[1], device_id_type=MESH)
         for step in range(1, z_size):
             pl.semaphore_signal(barrier, inc=1, device_id=z_id(step)[1], device_id_type=MESH)
@@ -175,10 +175,9 @@
     each(chips, for_core)
     each(chips, pair)
 
-    term[...] = dot(feats[chip, my_rows], two_send[chip], ((0,), (0,)))
-
     def arrive(piece):
         rows = pl.ds(piece * half, half)
+        term[rows] = dot(feats[chip, my_rows, rows], two_send[chip], ((0,), (0,)))
 
         def from_chip(step):
             q = other_chip(step)
@@ -224,6 +223,13 @@
         q = other_chip(step)
         two_copy(q, chip).start()
 
+    def sent():
+        for piece in range(2):
+            each(chips - 1, lambda step: send_x(step, piece).wait_send())
+            each(chips, lambda step: pass_on(other_chip(step), piece).wait_send())
+        each(chips, lambda step: one_copy(other_chip(step)).wait_send())
+        each(chips - 1, lambda step: two_copy(other_chip(step), chip).wait_send())
+
     if reduce_in:
         share = half // plane
         scale = 1.0 / math.sqrt(nodes * blk_size * rep_size)
@@ -257,7 +263,6 @@
             wg_part[rows] = term[rows].astype(BF16)
             for step in range(1, plane):
                 rs_copy(piece, step).start()
-        each(chips - 1, second)
         for piece in range(2):
             total = term[rows_of(piece, place)]
             for step in range(1, plane):
@@ -266,6 +271,7 @@
             z_buf[piece, my_z] = total.astype(BF16)
             for step in range(1, z_size):
                 z_copy(piece, step, my_z).start()
+        each(chips - 1, second)
         forward()
         for piece in range(2):
             for step in range(1, z_size):
@@ -279,6 +285,13 @@
             if piece == 0:
                 activate()
         columns()
+        sent()
+        for piece in range(2):
+            for step in range(1, plane):
+                rs_copy(piece, step).wait_send()
+                ag_copy(piece, step, place).wait_send()
+            for step in range(1, z_size):
+                z_copy(piece, step, my_z).wait_send()
         for piece in range(2):
             for step in range(1, plane):
                 ag_copy(piece, step, lax.rem(place + plane - step, plane)).wait_recv()
@@ -292,19 +305,7 @@
         forward()
         activate()
         columns()
-
-    for piece in range(2):
-        each(chips - 1, lambda step: send_x(step, piece).wait_send())
-        each(chips, lambda step: pass_on(other_chip(step), piece).wait_send())
-    each(chips, lambda step: one_copy(other_chip(step)).wait_send())
-    each(chips - 1, lambda step: two_copy(other_chip(step), chip).wait_send())
-    if reduce_in:
-        for piece in range(2):
-            for step in range(1, plane):
-                rs_copy(piece, step).wait_send()
-                ag_copy(piece, step, place).wait_send()
-            for step in range(1, z_size):
-                z_copy(piece, step, my_z).wait_send()
+        sent()
 
 
 def write_out(a_ref, b_ref, c_ref, a_out, b_out, c_out, sem):

time: 23.3 us -> 23.1 us (level)
  no operation moved by 1% of the time
where the time goes in v5:
time: 23.1 us; the launch traced here: 23 us
  Pallas kernels  22.3 us (97%)
  between operations  0.64 us (3%)
    pallas_call x1, Pallas kernels, per_device(): pl.pallas_call(functools.partial(kernel, dims), out_shape=(jax.ShapeDtype...  21.5 us
    pallas_call x1, Pallas kernels, per_device(): pl.pallas_call(write_out, out_shape=tuple((jax.ShapeDtypeStruct(r.shape,...  0.82 us

profile of v5, /device:TPU:0, one launch (start us, length us, event | category | flops | bytes accessed | tf_op | source)
XLA Modules:
  0.0 23.0 jit_solution(14762448432885852061)
XLA Ops:
  0.6 21.5 %layer.1 = (bf16[256,256]{1,0:T(8,128)(2,1)S(1)}, bf16[256,256]{1,0:T(8,128)(2,1)S(1)}, f32[256,256]{1,0:T(8,128)S(1)}) custom-call(s32[2]{0:T(128)} %refs_0_.1, s32[2,8]{1,0:T(2,128)} %refs_1_.1, bf16[256,256]{1,0:T(8,128)(2,1)} %bitcast.6, bf16[2,8,128,128]{3,2,1,0:T(8,128)(2,1)} %refs_3_.1, bf16[256,256]{1,0:T(8,128)(2,1)} %bitcast.7, ...), custom_call_target="tpu_custom_call" | custom-call | tf_op jit(solution)/shard_map/layer/pallas_call | solution.py:364
  22.1 0.8 %write_out.1 = (bf16[256,256]{1,0:T(8,128)(2,1)}, bf16[256,256]{1,0:T(8,128)(2,1)}, f32[256,256]{1,0:T(8,128)}) custom-call(bf16[256,256]{1,0:T(8,128)(2,1)S(1)} %get-tuple-element.9.a_ref, bf16[256,256]{1,0:T(8,128)(2,1)S(1)} %get-tuple-element.10.b_ref, f32[256,256]{1,0:T(8,128)S(1)} %get-tuple-element.11.c_ref), custom_call_target="tpu_custom_call" | custom-call | tf_op jit(solution)/shard_map/write_out/pallas_call | solution.py:381

commit v6 on v5

--- a/solution.py
+++ b/solution.py
@@ -46,9 +46,15 @@
     def other_chip(step):
         return lax.rem(chip + 1 + step, chips)
 
-    def plane_id(step):
-        there = lax.rem(place + step, plane)
-        return there, {"blk": lax.rem(there, blk_size), "rep": my_z * plane_y + there // blk_size}
+    offsets = [(dy, dx, dc) for dy in range(plane_y) for dx in range(chips) for dc in range(2)][1:]
+    offsets.sort(key=lambda o: -2 * min(o[0], plane_y - o[0]) - 2 * min(o[1], chips - o[1]) - o[2])
+    steps = range(len(offsets))
+
+    def plane_id(step, back=1):
+        dy, dx, dc = offsets[step]
+        y = lax.rem(my_y + plane_y + back * dy, plane_y)
+        there = lax.rem(chip + chips + back * dx, chips) * 2 + (1 - core if dc else core)
+        return y * blk_size + there, {"blk": there, "rep": my_z * plane_y + y}
 
     def z_id(step):
         there = lax.rem(my_z + step, z_size)
@@ -56,7 +62,7 @@
 
     barrier = pltpu.get_barrier_semaphore()
     if reduce_in:
-        for step in sorted(range(1, plane), key=lambda s: min(s, plane - s)):
+        for step in reversed(steps):
             pl.semaphore_signal(barrier, inc=1, device_id=plane_id(step)[1], device_id_type=MESH)
         for step in range(1, z_size):
             pl.semaphore_signal(barrier, inc=1, device_id=z_id(step)[1], device_id_type=MESH)
@@ -187,11 +193,12 @@
 
         each(chips - 1, from_chip)
 
-    def forward():
+    def forward_own():
         for piece in range(2):
             passed(chip, piece).wait_recv()
         act[...] = dot(dense[chip], feats[chip], ((0,), (0,)))
 
+    def forward_others():
         def from_chip(step):
             q = other_chip(step)
             for piece in range(2):
@@ -240,8 +247,8 @@
         def rs_copy(piece, step):
             there, device = plane_id(step)
             return pltpu.make_async_remote_copy(
-                src_ref=wg_part.at[rows_of(piece, there)], dst_ref=rs_recv.at[piece, step - 1],
-                send_sem=rs_ssem.at[piece, step - 1], recv_sem=rs_rsem.at[piece, step - 1],
+                src_ref=wg_part.at[rows_of(piece, there)], dst_ref=rs_recv.at[piece, step],
+                send_sem=rs_ssem.at[piece, step], recv_sem=rs_rsem.at[piece, step],
                 device_id=device, device_id_type=MESH)
 
         def z_copy(piece, step, slot):
@@ -254,25 +261,26 @@
             rows = rows_of(piece, owner)
             return pltpu.make_async_remote_copy(
                 src_ref=wg_full.at[rows], dst_ref=wg_full.at[rows],
-                send_sem=ag_ssem.at[piece, step - 1], recv_sem=ag_rsem.at[piece, step - 1],
+                send_sem=ag_ssem.at[piece, step], recv_sem=ag_rsem.at[piece, step],
                 device_id=plane_id(step)[1], device_id_type=MESH)
 
         for piece in range(2):
             arrive(piece)
             rows = pl.ds(piece * half, half)
             wg_part[rows] = term[rows].astype(BF16)
-            for step in range(1, plane):
+            for step in steps:
                 rs_copy(piece, step).start()
+        forward_own()
         for piece in range(2):
             total = term[rows_of(piece, place)]
-            for step in range(1, plane):
+            for step in steps:
                 rs_copy(piece, step).wait_recv()
-                total = total + rs_recv[piece, step - 1].astype(F32)
+                total = total + rs_recv[piece, step].astype(F32)
             z_buf[piece, my_z] = total.astype(BF16)
             for step in range(1, z_size):
                 z_copy(piece, step, my_z).start()
         each(chips - 1, second)
-        forward()
+        forward_others()
         for piece in range(2):
             for step in range(1, z_size):
                 z_copy(piece, step, z_id(step)[0]).wait_recv()
@@ -280,21 +288,21 @@
             for z in range(1, z_size):
                 total = total + z_buf[piece, z].astype(F32)
             wg_full[rows_of(piece, place)] = (total * scale).astype(BF16)
-            for step in range(1, plane):
+            for step in steps:
                 ag_copy(piece, step, place).start()
             if piece == 0:
                 activate()
         columns()
         sent()
         for piece in range(2):
-            for step in range(1, plane):
+            for step in steps:
                 rs_copy(piece, step).wait_send()
                 ag_copy(piece, step, place).wait_send()
             for step in range(1, z_size):
                 z_copy(piece, step, my_z).wait_send()
         for piece in range(2):
-            for step in range(1, plane):
-                ag_copy(piece, step, lax.rem(place + plane - step, plane)).wait_recv()
+            for step in steps:
+                ag_copy(piece, step, plane_id(step, -1)[0]).wait_recv()
             rows = pl.ds(piece * half, half)
             wg_ref[rows] = wg_full[rows].astype(F32)
     else:
@@ -302,7 +310,8 @@
             arrive(piece)
         wg_ref[...] = term[...]
         each(chips - 1, second)
-        forward()
+        forward_own()
+        forward_others()
         activate()
         columns()
         sent()

time: 23.1 us -> 23.2 us (level)
  no operation moved by 1% of the time
where the time goes in v6:
time: 23.2 us; the launch traced here: 23.1 us
  Pallas kernels  22.4 us (97%)
  between operations  0.64 us (3%)
    pallas_call x1, Pallas kernels, per_device(): pl.pallas_call(functools.partial(kernel, dims), out_shape=(jax.ShapeDtype...  21.6 us
    pallas_call x1, Pallas kernels, per_device(): pl.pallas_call(write_out, out_shape=tuple((jax.ShapeDtypeStruct(r.shape,...  0.82 us

profile of v6, /device:TPU:0, one launch (start us, length us, event | category | flops | bytes accessed | tf_op | source)
XLA Modules:
  0.0 23.1 jit_solution(17474301158749897612)
XLA Ops:
  0.6 21.6 %layer.1 = (bf16[256,256]{1,0:T(8,128)(2,1)S(1)}, bf16[256,256]{1,0:T(8,128)(2,1)S(1)}, f32[256,256]{1,0:T(8,128)S(1)}) custom-call(s32[2]{0:T(128)} %refs_0_.1, s32[2,8]{1,0:T(2,128)} %refs_1_.1, bf16[256,256]{1,0:T(8,128)(2,1)} %bitcast.6, bf16[2,8,128,128]{3,2,1,0:T(8,128)(2,1)} %refs_3_.1, bf16[256,256]{1,0:T(8,128)(2,1)} %bitcast.7, ...), custom_call_target="tpu_custom_call" | custom-call | tf_op jit(solution)/shard_map/layer/pallas_call | solution.py:373
  22.3 0.8 %write_out.1 = (bf16[256,256]{1,0:T(8,128)(2,1)}, bf16[256,256]{1,0:T(8,128)(2,1)}, f32[256,256]{1,0:T(8,128)}) custom-call(bf16[256,256]{1,0:T(8,128)(2,1)S(1)} %get-tuple-element.9.a_ref, bf16[256,256]{1,0:T(8,128)(2,1)S(1)} %get-tuple-element.10.b_ref, f32[256,256]{1,0:T(8,128)S(1)} %get-tuple-element.11.c_ref), custom_call_target="tpu_custom_call" | custom-call | tf_op jit(solution)/shard_map/write_out/pallas_call | solution.py:390

commit v7 on v5

--- a/solution.py
+++ b/solution.py
@@ -29,7 +29,7 @@
     blk_size, rep_size, rows_per, slots, tile, width, plane_y, reduce_in = dims
     (count_hbm, cols_hbm, feat_ref, tv_ref, grad_ref, weight_ref, mask_ref) = refs[:7]
     (act_ref, col_ref, wg_ref) = refs[7:10]
-    (count_ref, cols_ref, mask, tv, grad, weight, feats, dense, own, one_send, one_recv, two_send, two_recv,
+    (count_ref, cols_ref, mask, tv, grad, weight, arrived, feats, dense, own, one_send, one_recv, two_send, two_recv,
      act, col, term, wg_part, rs_recv, z_buf, wg_full,
      in_sem, f_send, f_recv, fwd_send, one_ssem, one_rsem, two_ssem, two_rsem,
      rs_ssem, rs_rsem, z_ssem, z_rsem, ag_ssem, ag_rsem) = refs[10:]
@@ -74,7 +74,7 @@
         loads.append(pltpu.make_async_copy(tv_ref.at[t], tv.at[t, pl.ds(0, slots)], in_sem.at[2 + t]))
     my_rows = pl.ds(pl.multiple_of(core * nodes, nodes), nodes)
     sib_rows = pl.ds(pl.multiple_of((1 - core) * nodes, nodes), nodes)
-    loads.append(pltpu.make_async_copy(feat_ref, feats.at[chip, my_rows], in_sem.at[2 + rows_per]))
+    loads.append(pltpu.make_async_copy(feat_ref, arrived.at[chip], in_sem.at[2 + rows_per]))
     loads.append(pltpu.make_async_copy(count_hbm, count_ref, in_sem.at[3 + rows_per]))
     loads.append(pltpu.make_async_copy(cols_hbm, cols_ref, in_sem.at[4 + rows_per]))
     loads.append(pltpu.make_async_copy(mask_ref, mask, in_sem.at[5 + rows_per]))
@@ -85,7 +85,7 @@
     def x_copy(origin, device, piece):
         lanes = pl.ds(piece * half, half)
         return pltpu.make_async_remote_copy(
-            src_ref=feat_ref.at[:, lanes], dst_ref=feats.at[origin, my_rows, lanes],
+            src_ref=feat_ref.at[:, lanes], dst_ref=arrived.at[origin, :, lanes],
             send_sem=f_send.at[device // 2, piece], recv_sem=f_recv.at[0, origin, piece],
             device_id={"blk": device, "rep": rep}, device_id_type=MESH)
 
@@ -95,12 +95,17 @@
     def came_x(q, piece):
         return x_copy(q, q * 2 + core, piece)
 
-    def sib_copy(q, rows, piece):
-        lanes = pl.ds(piece * half, half)
+    def sib_copy(q, side, piece):
+        rows = pl.ds(piece * half, half)
         return pltpu.make_async_remote_copy(
-            src_ref=feats.at[q, rows, lanes], dst_ref=feats.at[q, rows, lanes],
+            src_ref=feats.at[q, rows, side], dst_ref=feats.at[q, rows, side],
             send_sem=fwd_send.at[q, piece], recv_sem=f_recv.at[1, q, piece],
             device_id={"blk": sib, "rep": rep}, device_id_type=MESH)
+
+    def turn(q, piece):
+        lanes = pl.ds(piece * half, half)
+        feats[q, lanes, my_rows] = arrived[q, :, lanes].T
+        pass_on(q, piece).start()
 
     def pass_on(q, piece):
         return sib_copy(q, my_rows, piece)
@@ -112,9 +117,6 @@
         each(chips - 1, lambda step: send_x(step, piece).start())
     loads[1].start()
     loads[5 + rows_per].start()
-    loads[2 + rows_per].wait()
-    for piece in range(2):
-        pass_on(chip, piece).start()
 
     loads[3 + rows_per].wait()
     loads[4 + rows_per].wait()
@@ -173,36 +175,39 @@
 
     each(chips, for_sibling)
     each(chips, for_core)
+    loads[2 + rows_per].wait()
+    for piece in range(2):
+        turn(chip, piece)
     each(chips, pair)
 
     def arrive(piece):
         rows = pl.ds(piece * half, half)
-        term[rows] = dot(feats[chip, my_rows, rows], two_send[chip], ((0,), (0,)))
+        term[rows] = dot(feats[chip, rows, my_rows], two_send[chip])
 
         def from_chip(step):
             q = other_chip(step)
             came_x(q, piece).wait_recv()
-            pass_on(q, piece).start()
-            term[rows] += dot(feats[q, my_rows, rows], two_send[q], ((0,), (0,)))
+            turn(q, piece)
+            term[rows] += dot(feats[q, rows, my_rows], two_send[q])
 
         each(chips - 1, from_chip)
 
     def forward():
         for piece in range(2):
             passed(chip, piece).wait_recv()
-        act[...] = dot(dense[chip], feats[chip], ((0,), (0,)))
+        act[...] = dot(feats[chip], dense[chip])
 
         def from_chip(step):
             q = other_chip(step)
             for piece in range(2):
                 passed(q, piece).wait_recv()
-            act[...] += dot(dense[q], feats[q], ((0,), (0,)))
+            act[...] += dot(feats[q], dense[q])
 
         each(chips - 1, from_chip)
 
     def activate():
         loads[1].wait()
-        act_ref[...] = jnp.maximum(dot(act[...].astype(BF16), weight[...]), 0.0).astype(BF16)
+        act_ref[...] = jnp.maximum(dot(act[...].astype(BF16), weight[...], ((0,), (0,))), 0.0).astype(BF16)
 
     def columns():
         col[...] = own[chip]
@@ -338,14 +343,15 @@
         vmem((rows_per, slots + 1, tile, tile), BF16),
         vmem(block, BF16),
         vmem((width, width), BF16),
-        vmem((chips, 2 * nodes, width), BF16),
+        vmem((chips,) + block, BF16),
+        vmem((chips, width, 2 * nodes), BF16),
         vmem((chips, 2 * nodes, nodes), BF16),
         vmem((chips,) + block, F32),
         vmem((chips,) + block, BF16),
         vmem((chips,) + block, BF16),
         vmem((chips,) + block, BF16),
         vmem((chips,) + block, BF16),
-        vmem(block, F32),
+        vmem((width, nodes), F32),
         vmem(block, F32),
         vmem((width, width), F32),
         vmem((width, width), BF16),

time: 23.1 us -> 23.2 us (level)
  no operation moved by 1% of the time
where the time goes in v7:
time: 23.2 us; the launch traced here: 23 us
  Pallas kernels  22.4 us (97%)
  between operations  0.64 us (3%)
    pallas_call x1, Pallas kernels, per_device(): pl.pallas_call(functools.partial(kernel, dims), out_shape=(jax.ShapeDtype...  21.6 us
    pallas_call x1, Pallas kernels, per_device(): pl.pallas_call(write_out, out_shape=tuple((jax.ShapeDtypeStruct(r.shape,...  0.82 us

profile of v7, /device:TPU:0, one launch (start us, length us, event | category | flops | bytes accessed | tf_op | source)
XLA Modules:
  0.0 23.0 jit_solution(13235917251589781562)
XLA Ops:
  0.6 21.6 %layer.1 = (bf16[256,256]{1,0:T(8,128)(2,1)S(1)}, bf16[256,256]{1,0:T(8,128)(2,1)S(1)}, f32[256,256]{1,0:T(8,128)S(1)}) custom-call(s32[2]{0:T(128)} %refs_0_.1, s32[2,8]{1,0:T(2,128)} %refs_1_.1, bf16[256,256]{1,0:T(8,128)(2,1)} %bitcast.6, bf16[2,8,128,128]{3,2,1,0:T(8,128)(2,1)} %refs_3_.1, bf16[256,256]{1,0:T(8,128)(2,1)} %bitcast.7, ...), custom_call_target="tpu_custom_call" | custom-call | tf_op jit(solution)/shard_map/layer/pallas_call | solution.py:370
  22.2 0.8 %write_out.1 = (bf16[256,256]{1,0:T(8,128)(2,1)}, bf16[256,256]{1,0:T(8,128)(2,1)}, f32[256,256]{1,0:T(8,128)}) custom-call(bf16[256,256]{1,0:T(8,128)(2,1)S(1)} %get-tuple-element.9.a_ref, bf16[256,256]{1,0:T(8,128)(2,1)S(1)} %get-tuple-element.10.b_ref, f32[256,256]{1,0:T(8,128)S(1)} %get-tuple-element.11.c_ref), custom_call_target="tpu_custom_call" | custom-call | tf_op jit(solution)/shard_map/write_out/pallas_call | solution.py:387

commit v8 on v7

--- a/solution.py
+++ b/solution.py
@@ -56,10 +56,10 @@
 
     barrier = pltpu.get_barrier_semaphore()
     if reduce_in:
-        for step in sorted(range(1, plane), key=lambda s: min(s, plane - s)):
+        for step in range(z_size - 1, 0, -1):
+            pl.semaphore_signal(barrier, inc=1, device_id=z_id(step)[1], device_id_type=MESH)
+        for step in sorted(range(1, plane), key=lambda s: -min(s, plane - s)):
             pl.semaphore_signal(barrier, inc=1, device_id=plane_id(step)[1], device_id_type=MESH)
-        for step in range(1, z_size):
-            pl.semaphore_signal(barrier, inc=1, device_id=z_id(step)[1], device_id_type=MESH)
         greeted = plane - 1 + z_size - 1
     else:
         pl.semaphore_signal(barrier, inc=1, device_id={"blk": sib, "rep": rep}, device_id_type=MESH)

time: 23.2 us -> 23.1 us (level)
  no operation moved by 1% of the time
where the time goes in v8:
time: 23.1 us; the launch traced here: 22.9 us
  Pallas kernels  22.3 us (97%)
  between operations  0.64 us (3%)
    pallas_call x1, Pallas kernels, per_device(): pl.pallas_call(functools.partial(kernel, dims), out_shape=(jax.ShapeDtype...  21.5 us
    pallas_call x1, Pallas kernels, per_device(): pl.pallas_call(write_out, out_shape=tuple((jax.ShapeDtypeStruct(r.shape,...  0.82 us

profile of v8, /device:TPU:0, one launch (start us, length us, event | category | flops | bytes accessed | tf_op | source)
XLA Modules:
  0.0 22.9 jit_solution(8146743409391249617)
XLA Ops:
  0.6 21.5 %layer.1 = (bf16[256,256]{1,0:T(8,128)(2,1)S(1)}, bf16[256,256]{1,0:T(8,128)(2,1)S(1)}, f32[256,256]{1,0:T(8,128)S(1)}) custom-call(s32[2]{0:T(128)} %refs_0_.1, s32[2,8]{1,0:T(2,128)} %refs_1_.1, bf16[256,256]{1,0:T(8,128)(2,1)} %bitcast.6, bf16[2,8,128,128]{3,2,1,0:T(8,128)(2,1)} %refs_3_.1, bf16[256,256]{1,0:T(8,128)(2,1)} %bitcast.7, ...), custom_call_target="tpu_custom_call" | custom-call | tf_op jit(solution)/shard_map/layer/pallas_call | solution.py:370
  22.1 0.8 %write_out.1 = (bf16[256,256]{1,0:T(8,128)(2,1)}, bf16[256,256]{1,0:T(8,128)(2,1)}, f32[256,256]{1,0:T(8,128)}) custom-call(bf16[256,256]{1,0:T(8,128)(2,1)S(1)} %get-tuple-element.9.a_ref, bf16[256,256]{1,0:T(8,128)(2,1)S(1)} %get-tuple-element.10.b_ref, f32[256,256]{1,0:T(8,128)S(1)} %get-tuple-element.11.c_ref), custom_call_target="tpu_custom_call" | custom-call | tf_op jit(solution)/shard_map/write_out/pallas_call | solution.py:387
